TPU v7x, 128 devices: a whole 4x4x4 slice. The times are simulated.
128 devices in a mesh: dp: 16 (over x, z_lo, core), center: 8 (over z_hi, y).
Axes of the slice: x: 4, y: 4, z: 4 (z_hi: 2, z_lo: 2; z = z_hi * 2 + z_lo), core: 2. Of those that a mesh axis runs over, the one named last changes fastest.
Arguments:
- points: bfloat16 [24576, 128], P('dp'), may hold values from -1.5 to 1.5, as said below
- centers: bfloat16 [65536, 128], P('center'), may hold values from -1.5 to 1.5, as said below
- direction: float32 [65536, 128], P('center'), may hold values from -4 to 4, as said below
Outputs:
- product: float32 [65536, 128], P('center')
Inputs may be any that keep to these rules, and one draw needn't show every extreme that they name: Every row of points has a squared length of 128 up to bfloat16 rounding. Every row of centers has a squared length of 128 up to bfloat16 rounding. Every column of direction sums to zero.
All inputs are finite; a program needn't handle non-finite values.
Results may differ from a plain program's by a relative error of at most 0.003.
Values may be sent and summed in bfloat16 or wider, within the bound.
No kernel may reach another device: no remote copies, remote signals or barrier semaphores. Data moves between devices by JAX's collectives and lax.ppermute only.
A program may use at most 128 MiB of HBM per device.

v0:
```python
import jax
import jax.numpy as jnp
from jax import lax
from jax.sharding import PartitionSpec as P

CENTERS = 65536


width_scale = 6.4


def kernel_tile(pts, cens, cen_sq, gamma, amp):
    pts_sq = jnp.sum(pts.astype(jnp.float32) ** 2, axis=1)
    cross = jnp.dot(pts, cens.T, preferred_element_type=jnp.float32)
    dist = pts_sq[:, None] + cen_sq[None, :] - 2.0 * cross
    return jnp.exp(amp - gamma * dist).astype(jnp.bfloat16)


def per_device(points, centers, direction):
    rows, width = points.shape
    outputs = direction.shape[1]
    gamma = width_scale / width
    amp = 0.5 * width * jnp.log1p(4.0 * width_scale / width)
    cen_sq = jnp.sum(centers.astype(jnp.float32) ** 2, axis=1)
    dir_b = direction.astype(jnp.bfloat16)
    block = min(512, rows)
    blocks = points.reshape(rows // block, block, width)

    def forward(pts):
        kernel = kernel_tile(pts, centers, cen_sq, gamma, amp)
        return (kernel, jnp.dot(kernel, dir_b, preferred_element_type=jnp.float32))

    kernels, partial_fit = lax.map(forward, blocks)
    fitted = lax.psum(partial_fit.reshape(rows, outputs), "center")
    fitted_b = (fitted / jnp.sqrt(jnp.float32(CENTERS))).astype(jnp.bfloat16)
    total_points = rows * lax.axis_size("dp")
    fit_blocks = fitted_b.reshape(rows // block, block, outputs)
    partial_cols = jnp.einsum(
        "bnm,bnp->mp", kernels, fit_blocks, preferred_element_type=jnp.float32
    )
    summed = lax.psum(partial_cols, "dp")
    return summed / jnp.sqrt(jnp.float32(total_points))


def solution(mesh):
    return jax.shard_map(
        per_device,
        mesh=mesh,
        in_specs=(P("dp", None), P("center", None), P("center", None)),
        out_specs=P("center", None),
        check_vma=False,
    )
```

profile of v0, /device:TPU:1, one launch (start us, length us, event | category | flops | bytes accessed | tf_op | source)
XLA Modules:
  0.0 292.1 jit_solution(6608799809241450854)
XLA Ops:
  6.5 0.0 copy-start
  6.5 0.0 all-reduce.3.cloned.1.call-start
  6.5 2.4 convert_element_type.20
  9.0 2.7 multiply_reduce_fusion.1
  11.7 0.0 copy-done
  11.7 35.9 %while.13 = (s32[]{:T(128)}, bf16[3,512,8192]{2,1,0:T(8,128)(2,1)}, f32[3,512,128]{2,1,0:T(8,128)}, bf16[3,512,128]{2,1,0:T(8,128)(2,1)S(1)}, f32[8192]{0:T(1024...) while((s32[]{:T(128)}, bf16[3,512,8192]{2,1,0:T(8,128)(2,1)}, ...), condition=%wide.region_3.4_spmd, body=%wide.region_1.3_spmd.sunk | while | flops 2172845568 | bytes 29922904 | solution.py:33
  11.8 0.2 multiply_reduce_fusion.3
  11.9 8.8 %bitcast_dynamic-update-slice_fusion.2 = (bf16[3,512,8192]{2,1,0:T(8,128)(2,1)}, bf16[512,8192]{1,0:T(8,128)(2,1)S(1)}) fusion(bf16[3,512,8192]{2,1,0:T(8,128)(2,1)} %get-tuple-element.143, s32[]{:T(128)} %get-tuple-element.142, bf16[8192,128]{1,0:T(8,128)(2,1)} %get-tuple-element.155, bf16[3,512,128]{2,1,0:T(8,128)(2,1)S(1)} %get-tuple-element.153, ...), kind=kOutput, calls=%fused_computation.1.clone.1 | convolution fusion | flops 1098907648 | bytes 19041280 | tf_op jit(solution)/shard_map/while/body/eval_jaxpr/dot_general | solution.py:14
  20.7 3.0 %fusion.16 = f32[3,512,128]{2,1,0:T(8,128)} fusion(f32[3,512,128]{2,1,0:T(8,128)} %get-tuple-element.144, s32[]{:T(128)} %get-tuple-element.142, bf16[512,8192]{1,0:T(8,128)(2,1)S(1)} %get-tuple-element.133, bf16[8192,128]{1,0:T(8,128)(2,1)S(1)} %get-tuple-element.156), kind=kOutput, calls=%fused_computation.3.clone.1 | convolution fusion | flops 1073741824 | bytes 10748416 | tf_op jit(solution)/shard_map/while/body/eval_jaxpr/dot_general | solution.py:31
  23.7 0.1 multiply_reduce_fusion.3
  23.9 8.8 %bitcast_dynamic-update-slice_fusion.2 = (bf16[3,512,8192]{2,1,0:T(8,128)(2,1)}, bf16[512,8192]{1,0:T(8,128)(2,1)S(1)}) fusion(bf16[3,512,8192]{2,1,0:T(8,128)(2,1)} %get-tuple-element.143, s32[]{:T(128)} %get-tuple-element.142, bf16[8192,128]{1,0:T(8,128)(2,1)} %get-tuple-element.155, bf16[3,512,128]{2,1,0:T(8,128)(2,1)S(1)} %get-tuple-element.153, ...), kind=kOutput, calls=%fused_computation.1.clone.1 | convolution fusion | flops 1098907648 | bytes 19041280 | tf_op jit(solution)/shard_map/while/body/eval_jaxpr/dot_general | solution.py:14
  32.7 3.0 %fusion.16 = f32[3,512,128]{2,1,0:T(8,128)} fusion(f32[3,512,128]{2,1,0:T(8,128)} %get-tuple-element.144, s32[]{:T(128)} %get-tuple-element.142, bf16[512,8192]{1,0:T(8,128)(2,1)S(1)} %get-tuple-element.133, bf16[8192,128]{1,0:T(8,128)(2,1)S(1)} %get-tuple-element.156), kind=kOutput, calls=%fused_computation.3.clone.1 | convolution fusion | flops 1073741824 | bytes 10748416 | tf_op jit(solution)/shard_map/while/body/eval_jaxpr/dot_general | solution.py:31
  35.7 0.1 multiply_reduce_fusion.3
  35.8 8.8 %bitcast_dynamic-update-slice_fusion.2 = (bf16[3,512,8192]{2,1,0:T(8,128)(2,1)}, bf16[512,8192]{1,0:T(8,128)(2,1)S(1)}) fusion(bf16[3,512,8192]{2,1,0:T(8,128)(2,1)} %get-tuple-element.143, s32[]{:T(128)} %get-tuple-element.142, bf16[8192,128]{1,0:T(8,128)(2,1)} %get-tuple-element.155, bf16[3,512,128]{2,1,0:T(8,128)(2,1)S(1)} %get-tuple-element.153, ...), kind=kOutput, calls=%fused_computation.1.clone.1 | convolution fusion | flops 1098907648 | bytes 19041280 | tf_op jit(solution)/shard_map/while/body/eval_jaxpr/dot_general | solution.py:14
  44.6 3.0 %fusion.16 = f32[3,512,128]{2,1,0:T(8,128)} fusion(f32[3,512,128]{2,1,0:T(8,128)} %get-tuple-element.144, s32[]{:T(128)} %get-tuple-element.142, bf16[512,8192]{1,0:T(8,128)(2,1)S(1)} %get-tuple-element.133, bf16[8192,128]{1,0:T(8,128)(2,1)S(1)} %get-tuple-element.156), kind=kOutput, calls=%fused_computation.3.clone.1 | convolution fusion | flops 1073741824 | bytes 10748416 | tf_op jit(solution)/shard_map/while/body/eval_jaxpr/dot_general | solution.py:31
  47.7 0.0 all-reduce.3.cloned.1.call-update
  47.7 0.0 all-reduce.5.cloned.1.call-start
  47.8 84.9 %all-reduce.3.cloned.1.call-done = f32[1536,128]{1,0:T(8,128)} async-done(((f32[1536,128]{1,0:T(8,128)}), f32[1536,128]{1,0:T(8,128)}) %all-reduce.3.cloned.1.call-update) | async-done | bytes 786448 | tf_op jit(solution)/shard_map/psum | solution.py:34
  132.7 1.2 multiply_convert_fusion
  133.9 13.7 %convolution_bitcast_fusion.1 = f32[8192,128]{1,0:T(8,128)} fusion(bf16[3,512,8192]{2,1,0:T(8,128)(2,1)} %get-tuple-element.69, bf16[3,512,128]{2,1,0:T(8,128)(2,1)S(1)} %bitcast.36), kind=kOutput, calls=%fused_computation.8 | convolution fusion | flops 3221225472 | bytes 29753344 | tf_op jit(solution)/shard_map/bnm,bnp->mp/dot_general | solution.py:38
  147.5 0.0 all-reduce.5.cloned.1.call-update
  147.6 133.1 %all-reduce.5.cloned.1.call-done = f32[8192,128]{1,0:T(8,128)} async-done(((f32[8192,128]{1,0:T(8,128)}), f32[8192,128]{1,0:T(8,128)}) %all-reduce.5.cloned.1.call-update) | async-done | bytes 4194320 | tf_op jit(solution)/shard_map/psum | solution.py:41
  280.7 4.6 %broadcast_multiply_fusion = f32[8192,128]{1,0:T(8,128)} fusion(f32[8192,128]{1,0:T(8,128)} %all-reduce.5.cloned.1.call-done), kind=kLoop, calls=%fused_computation.10 | loop fusion | flops 1048576 | bytes 8388608 | tf_op jit(solution)/shard_map/div | solution.py:42
  (2 shorter events, 0.0 us)
Async XLA Ops:
  6.5 5.2 %copy-start = (bf16[1536,128]{1,0:T(8,128)(2,1)S(1)}, bf16[1536,128]{1,0:T(8,128)(2,1)}, u32[]{:S(2)}) copy-start(bf16[1536,128]{1,0:T(8,128)(2,1)} %param.5) | copy-start | bytes 1179652
  6.5 126.2 %all-reduce.3.cloned.1.call-start = ((), (), s32[]{:S(2)}) async-start(), calls=%async_computation | async-start | bytes 1572864 | tf_op jit(solution)/shard_map/psum | solution.py:34
  47.7 233.0 %all-reduce.5.cloned.1.call-start = ((), (), s32[]{:S(2)}) async-start(), calls=%async_computation.1 | async-start | bytes 8388608 | tf_op jit(solution)/shard_map/psum | solution.py:41
Sparse Core Ops, SparseCore 0:
  47.8 84.8 all-reduce.2
  147.7 132.9 all-reduce.4
where the time goes:
time: 292 us
  waiting for transfers between devices  218 us (75%)
  matrix products  49.1 us (17%)
  between operations  13.4 us (5%)
  other arithmetic  11.4 us (4%)
    psum x1, waiting for transfers between devices, per_device(): summed = lax.psum(partial_cols, 'dp')  133 us
    psum x1, waiting for transfers between devices, per_device(): fitted = lax.psum(partial_fit.reshape(rows, outputs), 'center')  84.9 us
    dot_general x3, matrix products, kernel_tile(): cross = jnp.dot(pts, cens.T, preferred_element_type=jnp.float32)  26.4 us
    dot_general x1, matrix products, per_device(): jnp.einsum('bnm,bnp->mp', kernels, fit_blocks, preferred_element_type=jnp...  13.7 us
    dot_general x3, matrix products, forward(): return (kernel, jnp.dot(kernel, dir_b, preferred_element_type=jnp.float32))  9.09 us
  transfers between devices with their start and end apart: 2, of which 2 were waited for; matrix products, arithmetic and copies ran while one was open for 0% of the time, Pallas kernels for 0%

commit v1 on v0

v1 whole, which is shorter than its diff:
```python
import functools
import math

import jax
import jax.numpy as jnp
from jax import lax
from jax.experimental import pallas as pl
from jax.experimental.pallas import tpu as pltpu
from jax.sharding import PartitionSpec as P

CENTERS = 65536
POINTS = 24576
WIDTH = 128
GAMMA = 6.4 / WIDTH
AMP = 0.5 * WIDTH * math.log1p(4.0 * GAMMA)
LOG2E = math.log2(math.e)
CROSS_SCALE = 2.0 * GAMMA * LOG2E
BF16 = jnp.bfloat16
F32 = jnp.float32
ROWS_BY_ROWS = (((1,), (1,)), ((), ()))


def split_bf16(x):
    high = x.astype(BF16)
    return high, (x - high.astype(F32)).astype(BF16)


def row_squares(x):
    x = x.astype(F32)
    return jnp.sum(x * x, axis=1, keepdims=True)


def fit_kernel(tile_rows, points_ref, centers_ref, direction_ref, tile_ref, fit_ref, scaled_ref, sum_ref):
    step = pl.program_id(0)
    rows = points_ref.shape[0]
    cols = centers_ref.shape[0]

    @pl.when(step == 0)
    def _():
        high, low = split_bf16(points_ref[...].astype(F32) * CROSS_SCALE)
        scaled_ref[:, :WIDTH] = high
        scaled_ref[:, WIDTH:] = low
        sum_ref[...] = jnp.zeros_like(sum_ref)

    chunk = 1024
    for part in range(cols // chunk):
        here = slice(part * chunk, (part + 1) * chunk)
        cens = centers_ref[here, :]
        factor = jnp.exp2(-GAMMA * LOG2E * row_squares(cens))
        high, low = split_bf16(direction_ref[here, :].astype(BF16).astype(F32) * factor)
        weights = jnp.concatenate([high, low], axis=1)
        twice = jnp.concatenate([cens, cens], axis=1)
        for t in range(rows // tile_rows):
            at = slice(t * tile_rows, (t + 1) * tile_rows)
            cross = lax.dot_general(scaled_ref[at, :], twice, ROWS_BY_ROWS, preferred_element_type=F32)
            tile = jnp.exp2(cross).astype(BF16)
            tile_ref[at, pl.ds(pl.multiple_of(step * cols + part * chunk, chunk), chunk)] = tile
            sum_ref[at, :] += jnp.dot(tile, weights, preferred_element_type=F32)

    @pl.when(step == pl.num_programs(0) - 1)
    def _():
        factor = jnp.exp2(2.0 * LOG2E * (AMP - GAMMA * row_squares(points_ref[...])))
        factor = factor * (1.0 / math.sqrt(CENTERS))
        fit_ref[...] = (sum_ref[:, :WIDTH] + sum_ref[:, WIDTH:]) * factor


def fit_call(points, centers, direction, cols=2048, tile_rows=256):
    rows, count = points.shape[0], centers.shape[0]
    return pl.pallas_call(
        functools.partial(fit_kernel, tile_rows),
        grid=(count // cols,),
        in_specs=[
            pl.BlockSpec((rows, WIDTH), lambda j: (0, 0)),
            pl.BlockSpec((cols, WIDTH), lambda j: (j, 0)),
            pl.BlockSpec((cols, WIDTH), lambda j: (j, 0)),
        ],
        out_specs=[
            pl.BlockSpec(memory_space=pltpu.VMEM),
            pl.BlockSpec((rows, WIDTH), lambda j: (0, 0)),
        ],
        out_shape=[pltpu.VMEM((rows, count), BF16), jax.ShapeDtypeStruct((rows, WIDTH), F32)],
        scratch_shapes=[pltpu.VMEM((rows, 2 * WIDTH), BF16), pltpu.VMEM((rows, 2 * WIDTH), F32)],
        compiler_params=pltpu.CompilerParams(vmem_limit_bytes=30 * 2**20),
        name="fit_tiles",
    )(points, centers, direction)


def back_kernel(half_ref, fitted_ref, centers_ref, tile_ref, out_ref, turned_ref):
    step = pl.program_id(0)
    cols = centers_ref.shape[0]
    half = half_ref[0]
    span = cols * pl.num_programs(0)

    @pl.when(step == 0)
    def _():
        turned_ref[...] = fitted_ref[...].astype(F32).T.astype(BF16)

    factor = jnp.exp2(-GAMMA * LOG2E * row_squares(centers_ref[...])) * (1.0 / math.sqrt(POINTS))
    tile = tile_ref[:, pl.ds(pl.multiple_of(half * span + step * cols, cols), cols)]
    out = jnp.dot(turned_ref[...], tile, preferred_element_type=F32).T
    out_ref[...] = (out * factor).astype(BF16)


def back_call(half, fitted, centers, tiles, cols=2048):
    rows, count = tiles.shape
    steps = count // 2 // cols
    tiles = pltpu.with_memory_space_constraint(tiles, pltpu.VMEM)
    return pl.pallas_call(
        back_kernel,
        grid_spec=pltpu.PrefetchScalarGridSpec(
            num_scalar_prefetch=1,
            grid=(steps,),
            in_specs=[
                pl.BlockSpec((rows, WIDTH), lambda j, half: (0, 0)),
                pl.BlockSpec((cols, WIDTH), lambda j, half: (half[0] * steps + j, 0)),
                pl.BlockSpec(memory_space=pltpu.VMEM),
            ],
            out_specs=pl.BlockSpec((cols, WIDTH), lambda j, half: (j, 0)),
            scratch_shapes=[pltpu.VMEM((WIDTH, rows), BF16)],
        ),
        out_shape=jax.ShapeDtypeStruct((count // 2, WIDTH), BF16),
        compiler_params=pltpu.CompilerParams(vmem_limit_bytes=16 * 2**20),
        name="back_tiles",
    )(half, fitted, centers, tiles)


def widen_kernel(core_ref, mine_ref, other_ref, out_ref):
    mine = pl.program_id(0) == core_ref[0]

    @pl.when(mine)
    def _():
        out_ref[...] = mine_ref[...].astype(F32)

    @pl.when(jnp.logical_not(mine))
    def _():
        out_ref[...] = other_ref[...].astype(F32)


def widen_call(core, mine, other, block=2048):
    count = mine.shape[0]
    steps = count // block
    return pl.pallas_call(
        widen_kernel,
        grid_spec=pltpu.PrefetchScalarGridSpec(
            num_scalar_prefetch=1,
            grid=(2, steps),
            in_specs=[
                pl.BlockSpec((block, WIDTH), lambda h, j, core: (jnp.where(h == core[0], j, 0), 0)),
                pl.BlockSpec((block, WIDTH), lambda h, j, core: (jnp.where(h == core[0], 0, j), 0)),
            ],
            out_specs=pl.BlockSpec((block, WIDTH), lambda h, j, core: (h * steps + j, 0)),
        ),
        out_shape=jax.ShapeDtypeStruct((2 * count, WIDTH), F32),
        name="widen",
    )(core, mine, other)


def per_device(points, centers, direction):
    rows, count = points.shape[0], centers.shape[0]
    dp, groups = lax.axis_size("dp"), lax.axis_size("center")
    core = lax.rem(lax.axis_index("dp"), 2)
    chips = dp // 2
    same_core = [[2 * chip + c for chip in range(chips)] for c in range(2)]
    swap = [(i, i ^ 1) for i in range(dp)]

    tiles, partial_fit = fit_call(points, centers, direction)
    part = rows // groups
    pieces = lax.all_to_all(partial_fit.reshape(groups, part, WIDTH), "center", 0, 0)
    fitted = jnp.sum(pieces, axis=0).astype(BF16)
    fitted = jnp.broadcast_to(fitted[None], (groups, part, WIDTH))
    fitted = lax.all_to_all(fitted, "center", 0, 0).reshape(rows, WIDTH)

    mine_id = core.astype(jnp.int32).reshape(1)
    theirs = back_call(1 - mine_id, fitted, centers, tiles)
    received = lax.ppermute(theirs, "dp", swap)
    mine = back_call(mine_id, fitted, centers, tiles)
    both = (mine.astype(F32) + received.astype(F32)).astype(BF16)
    part = count // 2 // chips
    pieces = lax.all_to_all(
        both.reshape(chips, part, WIDTH), "dp", 0, 0, axis_index_groups=same_core
    )
    summed = jnp.sum(pieces.astype(F32), axis=0).astype(BF16)
    summed = jnp.broadcast_to(summed[None], (chips, part, WIDTH))
    summed = lax.all_to_all(summed, "dp", 0, 0, axis_index_groups=same_core)
    summed = summed.reshape(count // 2, WIDTH)
    other = lax.ppermute(summed, "dp", swap)
    return widen_call(mine_id, summed, other)


def solution(mesh):
    return jax.shard_map(
        per_device,
        mesh=mesh,
        in_specs=(P("dp", None), P("center", None), P("center", None)),
        out_specs=P("center", None),
        check_vma=False,
    )
```

time: 292 us -> 123 us (0.42)
  waiting for transfers between devices: 218 us -> 11 us
  blocking collectives: 0 us -> 57.6 us
  matrix products: 49.1 us -> 0 us
  Pallas kernels: 0 us -> 26.7 us
  local copies, waits for them, and re-layouts: 0.01 us -> 18.4 us
  between operations: 13.4 us -> 0.07 us
  other arithmetic: 11.4 us -> 0.46 us
  starting transfers between devices: 0.04 us -> 8.75 us
    psum x2 -> x0, waiting for transfers between devices: 218 us -> none  [the longest x1 133 us: per_device(): summed = lax.psum(partial_cols, 'dp')]
    all_to_all x0 -> x3, blocking collectives: none -> 57.6 us  [the longest x1 21.9 us: per_device(): lax.all_to_all(partial_fit.reshape(groups, part, WIDTH), 'center', 0, 0)]
    dot_general x7 -> x0, matrix products: 49.1 us -> none  [the longest x3 26.4 us: kernel_tile(): cross = jnp.dot(pts, cens.T, preferred_element_type=jnp.float32)]
    pallas_call x0 -> x4, Pallas kernels: none -> 26.7 us  [the longest x1 17.5 us: fit_call(): pl.pallas_call(functools.partial(fit_kernel, tile_rows), grid=(count // c...]
    unnamed x2 -> x10, local copies, waits for them, and re-layouts: 0.01 us -> 17.5 us
    all_to_all x0 -> x1, waiting for transfers between devices: none -> 8.74 us  [per_device(): fitted = lax.all_to_all(fitted, 'center', 0, 0).reshape(rows, WIDTH)]
    ppermute x0 -> x2, starting transfers between devices: none -> 5.3 us  [the longest x1 2.67 us: per_device(): other = lax.ppermute(summed, 'dp', swap)]
    div x1 -> x0, other arithmetic: 4.56 us -> none  [per_device(): return summed / jnp.sqrt(jnp.float32(total_points))]
  transfers between devices with their start and end apart: 2 -> 3, of which waited for: 2 -> 2; matrix products, arithmetic and copies ran while one was open for 0% -> 0% of each run, Pallas kernels for 0% -> 2%
where the time goes in v1:
time: 123 us
  blocking collectives  57.6 us (47%)
  Pallas kernels  26.7 us (22%)
  local copies, waits for them, and re-layouts  18.4 us (15%)
  waiting for transfers between devices  11 us (9%)
  starting transfers between devices  8.75 us (7%)
    all_to_all x1, blocking collectives, per_device(): lax.all_to_all(partial_fit.reshape(groups, part, WIDTH), 'center', 0, 0)  21.9 us
    all_to_all x1, blocking collectives, per_device(): lax.all_to_all(both.reshape(chips, part, WIDTH), 'dp', 0, 0, axis_index_g...  18.6 us
    pallas_call x1, Pallas kernels, fit_call(): pl.pallas_call(functools.partial(fit_kernel, tile_rows), grid=(count // c...  17.5 us
    unnamed x10, local copies, waits for them, and re-layouts  17.5 us
    all_to_all x1, blocking collectives, per_device(): summed = lax.all_to_all(summed, 'dp', 0, 0, axis_index_groups=same_core)  17 us
    all_to_all x1, waiting for transfers between devices, per_device(): fitted = lax.all_to_all(fitted, 'center', 0, 0).reshape(rows, WIDTH)  8.74 us
    pallas_call x2, Pallas kernels, back_call(): pl.pallas_call(back_kernel, grid_spec=pltpu.PrefetchScalarGridSpec(num_sc...  4.77 us
    pallas_call x1, Pallas kernels, widen_call(): pl.pallas_call(widen_kernel, grid_spec=pltpu.PrefetchScalarGridSpec(num_s...  4.37 us
  transfers between devices with their start and end apart: 3, of which 2 were waited for; matrix products, arithmetic and copies ran while one was open for 0% of the time, Pallas kernels for 2%

profile of v1, /device:TPU:1, one launch (start us, length us, event | category | flops | bytes accessed | tf_op | source)
XLA Modules:
  0.0 122.9 jit_solution(10684594552725047797)
XLA Ops:
  0.0 17.5 %fit_tiles.1 = (bf16[1536,8192]{1,0:T(8,128)(2,1)S(1)}, f32[1536,128]{1,0:T(8,128)}) custom-call(bf16[1536,128]{1,0:T(8,128)(2,1)} %points_ref.1, bf16[8192,128]{1,0:T(8,128)(2,1)} %centers_ref.5, f32[8192,128]{1,0:T(8,128)} %direction_ref.1), custom_call_target="tpu_custom_call" | custom-call | tf_op jit(solution)/shard_map/fit_tiles/pallas_call | solution.py:69
  17.5 0.0 copy-start
  17.5 8.3 %copy-done = bf16[1536,8192]{1,0:T(8,128)(2,1)} copy-done((bf16[1536,8192]{1,0:T(8,128)(2,1)}, bf16[1536,8192]{1,0:T(8,128)(2,1)S(1)}, u32[]{:S(2)}) %copy-start) | copy-done | bytes 25165848
  25.8 0.0 copy-start.2
  25.8 21.9 %all_to_all.20 = f32[8,192,128]{2,1,0:T(8,128)S(1)} all-to-all(f32[8,192,128]{2,1,0:T(8,128)} %bitcast.10), channel_id=1, replica_groups=mesh['dp'=16,'center'=8] {'center'}, dimensions={0} | all-to-all | bytes 1572864 | tf_op jit(solution)/shard_map/all_to_all | solution.py:168
  47.8 0.8 broadcast_in_dim.4
  48.6 3.5 %all-to-all-start.1 = ((bf16[8,192,128]{2,1,0:T(8,128)(2,1)}), bf16[8,192,128]{2,1,0:T(8,128)(2,1)S(1)}, u32[]{:S(2)}, u32[]{:S(2)}) async-start(bf16[8,192,128]{2,1,0:T(8,128)(2,1)} %broadcast_in_dim.4), calls=%async_computation.1 | async-start | bytes 786432 | tf_op jit(solution)/shard_map/all_to_all | solution.py:171
  52.1 8.7 %all-to-all-done.1 = bf16[8,192,128]{2,1,0:T(8,128)(2,1)S(1)} async-done(((bf16[8,192,128]{2,1,0:T(8,128)(2,1)}), bf16[8,192,128]{2,1,0:T(8,128)(2,1)S(1)}, u32[]{:S(2)}, u32[]{:S(2)}) %all-to-all-start.1) | async-done | bytes 393248 | tf_op jit(solution)/shard_map/all_to_all | solution.py:171
  60.8 0.0 copy-done.2
  60.8 0.0 copy-start.1
  60.8 8.2 %copy-done.1 = bf16[1536,8192]{1,0:T(8,128)(2,1)S(1)} copy-done((bf16[1536,8192]{1,0:T(8,128)(2,1)S(1)}, bf16[1536,8192]{1,0:T(8,128)(2,1)}, u32[]{:S(2)}) %copy-start.1) | copy-done | bytes 25165848
  69.0 2.4 %back_tiles.3 = bf16[4096,128]{1,0:T(8,128)(2,1)S(1)} custom-call(s32[1]{0:T(128)S(6)} %sub.3.half_ref, bf16[1536,128]{1,0:T(8,128)(2,1)S(1)} %bitcast.5, bf16[8192,128]{1,0:T(8,128)(2,1)S(1)} %copy-done.2, bf16[1536,8192]{1,0:T(8,128)(2,1)S(1)} %copy-done.1), custom_call_target="tpu_custom_call" | custom-call | tf_op jit(solution)/shard_map/back_tiles/pallas_call | solution.py:108
  71.4 2.6 %collective-permute-start = (bf16[4096,128]{1,0:T(8,128)(2,1)S(1)}, bf16[4096,128]{1,0:T(8,128)(2,1)S(1)}, u32[]{:S(2)}, u32[]{:S(2)}) collective-permute-start(bf16[4096,128]{1,0:T(8,128)(2,1)S(1)} %back_tiles.3), channel_id=1, source_target_pairs={{0,8},{8,0},{16,24},{24,16},{32,40},{40,32},{48,56},{56,48},{64,72... | collective-permute-start | bytes 3145736 | tf_op jit(solution)/shard_map/ppermute | solution.py:175
  74.0 2.4 %back_tiles.2 = bf16[4096,128]{1,0:T(8,128)(2,1)S(1)} custom-call(s32[1]{0:T(128)} %bitcast.half_ref.core_ref, bf16[1536,128]{1,0:T(8,128)(2,1)S(1)} %bitcast.6, bf16[8192,128]{1,0:T(8,128)(2,1)S(1)} %copy-done.2, bf16[1536,8192]{1,0:T(8,128)(2,1)S(1)} %copy-done.1), custom_call_target="tpu_custom_call" | custom-call | tf_op jit(solution)/shard_map/back_tiles/pallas_call | solution.py:108
  76.4 0.0 collective-permute-done
  76.4 0.3 add_convert_fusion
  76.7 18.6 %all_to_all.21 = bf16[8,512,128]{2,1,0:T(8,128)(2,1)S(1)} all-to-all(bf16[8,512,128]{2,1,0:T(8,128)(2,1)S(1)} %bitcast.9), channel_id=1, replica_groups={{0,16,32,48,64,80,96,112},{8,24,40,56,72,88,104,120},{1,17,33,49,65,81,..., dimensions={0} | all-to-all | bytes 2097152 | tf_op jit(solution)/shard_map/all_to_all | solution.py:179
  95.3 0.1 reduce_sum.22
  95.5 0.1 broadcast_in_dim.5
  95.6 17.0 %all_to_all.22 = bf16[8,512,128]{2,1,0:T(8,128)(2,1)S(1)} all-to-all(bf16[8,512,128]{2,1,0:T(8,128)(2,1)S(1)} %broadcast_in_dim.5), channel_id=1, replica_groups={{0,16,32,48,64,80,96,112},{8,24,40,56,72,88,104,120},{1,17,33,49,65,81,..., dimensions={0} | all-to-all | bytes 2097152 | tf_op jit(solution)/shard_map/all_to_all | solution.py:184
  112.6 0.0 copy-start.3
  112.6 2.7 %collective-permute-start.1 = (bf16[4096,128]{1,0:T(8,128)(2,1)S(1)}, bf16[4096,128]{1,0:T(8,128)(2,1)S(1)}, u32[]{:S(2)}, u32[]{:S(2)}) collective-permute-start(bf16[4096,128]{1,0:T(8,128)(2,1)S(1)} %bitcast.7), channel_id=1, source_target_pairs={{0,8},{8,0},{16,24},{24,16},{32,40},{40,32},{48,56},{56,48},{64,72... | collective-permute-start | bytes 3145736 | tf_op jit(solution)/shard_map/ppermute | solution.py:186
  115.3 2.3 %collective-permute-done.1.other_ref = bf16[4096,128]{1,0:T(8,128)(2,1)S(1)} collective-permute-done((bf16[4096,128]{1,0:T(8,128)(2,1)S(1)}, bf16[4096,128]{1,0:T(8,128)(2,1)S(1)}, u32[]{:S(2)}, u32[]{:S(2)}) %collective-permute-start.1) | collective-permute-done | bytes 1048608 | tf_op jit(solution)/shard_map/ppermute | solution.py:186
  117.6 0.0 copy-done.3
  117.6 0.0 copy-start.4
  117.6 1.0 copy-done.4
  118.6 4.4 %widen.1 = f32[8192,128]{1,0:T(8,128)} custom-call(s32[1]{0:T(128)} %bitcast.half_ref.core_ref, bf16[4096,128]{1,0:T(8,128)(2,1)} %bitcast.8, bf16[4096,128]{1,0:T(8,128)(2,1)} %copy-done.4), custom_call_target="tpu_custom_call" | custom-call | tf_op jit(solution)/shard_map/widen/pallas_call | solution.py:142
  (1 shorter events, 0.0 us)
Async XLA Ops:
  17.5 8.3 %copy-start = (bf16[1536,8192]{1,0:T(8,128)(2,1)}, bf16[1536,8192]{1,0:T(8,128)(2,1)S(1)}, u32[]{:S(2)}) copy-start(bf16[1536,8192]{1,0:T(8,128)(2,1)S(1)} %get-tuple-element.8.tile_ref) | copy-start | bytes 75497472
  25.8 35.0 %copy-start.2 = (bf16[8192,128]{1,0:T(8,128)(2,1)S(1)}, bf16[8192,128]{1,0:T(8,128)(2,1)}, u32[]{:S(2)}) copy-start(bf16[8192,128]{1,0:T(8,128)(2,1)} %centers_ref.5) | copy-start | bytes 6291460
  48.6 12.2 %all-to-all-start.1 = ((bf16[8,192,128]{2,1,0:T(8,128)(2,1)}), bf16[8,192,128]{2,1,0:T(8,128)(2,1)S(1)}, u32[]{:S(2)}, u32[]{:S(2)}) async-start(bf16[8,192,128]{2,1,0:T(8,128)(2,1)} %broadcast_in_dim.4), calls=%async_computation.1 | async-start | bytes 786432 | tf_op jit(solution)/shard_map/all_to_all | solution.py:171
  60.8 8.2 %copy-start.1 = (bf16[1536,8192]{1,0:T(8,128)(2,1)S(1)}, bf16[1536,8192]{1,0:T(8,128)(2,1)}, u32[]{:S(2)}) copy-start(bf16[1536,8192]{1,0:T(8,128)(2,1)} %copy-done) | copy-start | bytes 75497472
  71.4 5.0 %collective-permute-start = (bf16[4096,128]{1,0:T(8,128)(2,1)S(1)}, bf16[4096,128]{1,0:T(8,128)(2,1)S(1)}, u32[]{:S(2)}, u32[]{:S(2)}) collective-permute-start(bf16[4096,128]{1,0:T(8,128)(2,1)S(1)} %back_tiles.3), channel_id=1, source_target_pairs={{0,8},{8,0},{16,24},{24,16},{32,40},{40,32},{48,56},{56,48},{64,72... | collective-permute-start | bytes 3145736 | tf_op jit(solution)/shard_map/ppermute | solution.py:175
  112.6 5.0 %copy-start.3 = (bf16[8,512,128]{2,1,0:T(8,128)(2,1)}, bf16[8,512,128]{2,1,0:T(8,128)(2,1)S(1)}, u32[]{:S(2)}) copy-start(bf16[8,512,128]{2,1,0:T(8,128)(2,1)S(1)} %all_to_all.22) | copy-start | bytes 3145732
  112.6 5.0 %collective-permute-start.1 = (bf16[4096,128]{1,0:T(8,128)(2,1)S(1)}, bf16[4096,128]{1,0:T(8,128)(2,1)S(1)}, u32[]{:S(2)}, u32[]{:S(2)}) collective-permute-start(bf16[4096,128]{1,0:T(8,128)(2,1)S(1)} %bitcast.7), channel_id=1, source_target_pairs={{0,8},{8,0},{16,24},{24,16},{32,40},{40,32},{48,56},{56,48},{64,72... | collective-permute-start | bytes 3145736 | tf_op jit(solution)/shard_map/ppermute | solution.py:186
  117.6 1.0 copy-start.4

commit v2 on v0

v2 whole, which is shorter than its diff:
```python
import functools
import math

import jax
import jax.numpy as jnp
from jax import lax
from jax.experimental import pallas as pl
from jax.experimental.pallas import tpu as pltpu
from jax.sharding import PartitionSpec as P

CENTERS = 65536
POINTS = 24576
WIDTH = 128
GAMMA = 6.4 / WIDTH
AMP = 0.5 * WIDTH * math.log1p(4.0 * GAMMA)
LOG2E = math.log2(math.e)
CROSS_SCALE = 2.0 * GAMMA * LOG2E
BF16 = jnp.bfloat16
F32 = jnp.float32
ROWS_BY_ROWS = (((1,), (1,)), ((), ()))


def split_bf16(x):
    high = x.astype(BF16)
    return high, (x - high.astype(F32)).astype(BF16)


def row_squares(x):
    x = x.astype(F32)
    return jnp.sum(x * x, axis=1, keepdims=True)


VMEM = pl.BlockSpec(memory_space=pltpu.VMEM)

OFFSETS = ((0, 2, 5, 7), (4, 1, 3, 6))
SETS = len(OFFSETS[0])
PACKED = [sum(k << (4 * j) for j, k in enumerate(row)) for row in OFFSETS]


def owner(me, j, other):
    table = jnp.where((me & 1) == other, PACKED[0], PACKED[1])
    return (me >> 1) ^ ((table >> (4 * j)) & 7)


def exchange(x, j):
    pairs = [
        (2 * chip + c, 2 * (chip ^ OFFSETS[c][j]) + c)
        for chip in range(8)
        for c in range(2)
        if OFFSETS[c][j]
    ]
    return lax.ppermute(x, "dp", pairs)


def on_chip(x):
    return pltpu.with_memory_space_constraint(x, pltpu.VMEM)


def in_hbm(x):
    return pltpu.with_memory_space_constraint(x, pltpu.HBM)


def fit_kernel(tile_rows, points_ref, centers_ref, direction_ref, tile_ref, fit_ref, scaled_ref, turned_ref, weights_ref, sum_ref):
    step = pl.program_id(0)
    rows = points_ref.shape[0]
    cols = centers_ref.shape[0]

    @pl.when(step == 0)
    def _():
        high, low = split_bf16(points_ref[...].astype(F32) * CROSS_SCALE)
        scaled_ref[:, :WIDTH] = high
        scaled_ref[:, WIDTH:] = low
        sum_ref[...] = jnp.zeros_like(sum_ref)

    turned = centers_ref[...].astype(F32).T
    shift = jnp.sum(turned * turned, axis=0, keepdims=True) * (-GAMMA * LOG2E)
    turned = turned.astype(BF16)
    turned_ref[:WIDTH, :] = turned
    turned_ref[WIDTH:, :] = turned
    weights_ref[...] = direction_ref[...].astype(BF16)

    def make(t):
        at = slice(t * tile_rows, (t + 1) * tile_rows)
        cross = jnp.dot(scaled_ref[at, :], turned_ref[...], preferred_element_type=F32)
        tile = jnp.exp2(cross + shift).astype(BF16)
        tile_ref[at, pl.ds(pl.multiple_of(step * cols, cols), cols)] = tile
        return tile

    def fit(t, tile):
        at = slice(t * tile_rows, (t + 1) * tile_rows)
        sum_ref[at, :] += jnp.dot(tile, weights_ref[...], preferred_element_type=F32)

    count = rows // tile_rows
    last = make(0)
    for t in range(1, count):
        tile = make(t)
        fit(t - 1, last)
        last = tile
    fit(count - 1, last)

    @pl.when(step == pl.num_programs(0) - 1)
    def _():
        factor = jnp.exp2(2.0 * LOG2E * (AMP - GAMMA * row_squares(points_ref[...])))
        fit_ref[...] = sum_ref[...] * (factor * (1.0 / math.sqrt(CENTERS)))


def fit_call(points, centers, direction, cols=2048, tile_rows=256):
    rows, count = points.shape[0], centers.shape[0]
    return pl.pallas_call(
        functools.partial(fit_kernel, tile_rows),
        grid=(count // cols,),
        in_specs=[
            pl.BlockSpec((rows, WIDTH), lambda j: (0, 0)),
            pl.BlockSpec((cols, WIDTH), lambda j: (j, 0)),
            pl.BlockSpec((cols, WIDTH), lambda j: (j, 0)),
        ],
        out_specs=[VMEM, VMEM],
        out_shape=[pltpu.VMEM((rows, count), BF16), pltpu.VMEM((rows, WIDTH), F32)],
        scratch_shapes=[
            pltpu.VMEM((rows, 2 * WIDTH), BF16),
            pltpu.VMEM((2 * WIDTH, cols), BF16),
            pltpu.VMEM((cols, WIDTH), BF16),
            pltpu.VMEM((rows, WIDTH), F32),
        ],
        compiler_params=pltpu.CompilerParams(vmem_limit_bytes=30 * 2**20),
        name="fit_tiles",
    )(points, centers, direction)


def back_kernel(other, first, fitted_ref, tile_ref, out_ref, turned_ref):
    step = pl.program_id(0)
    cols = out_ref.shape[0] // pl.num_programs(0)

    @pl.when(step == 0)
    def _():
        turned = fitted_ref[...].astype(F32).T * (1.0 / math.sqrt(POINTS))
        turned_ref[...] = turned.astype(BF16)

    piece = owner(lax.axis_index("dp"), first + step, other)
    tile = tile_ref[:, pl.ds(pl.multiple_of(piece * cols, cols), cols)]
    out = jnp.dot(turned_ref[...], tile, preferred_element_type=F32).T
    out_ref[pl.ds(pl.multiple_of(step * cols, cols), cols), :] = out.astype(BF16)


def back_call(fitted, tiles, other, first, number):
    rows, count = tiles.shape
    return pl.pallas_call(
        functools.partial(back_kernel, other, first),
        grid=(number,),
        in_specs=[VMEM, VMEM],
        out_specs=VMEM,
        out_shape=pltpu.VMEM((number * count // 8, WIDTH), BF16),
        scratch_shapes=[pltpu.VMEM((WIDTH, rows), BF16)],
        compiler_params=pltpu.CompilerParams(vmem_limit_bytes=30 * 2**20),
        name="back_tiles",
    )(on_chip(fitted), on_chip(tiles))


def sum_kernel(in_ref, out_ref):
    total = in_ref[0].astype(F32)
    for k in range(1, in_ref.shape[0]):
        total += in_ref[k].astype(F32)
    total = total.astype(BF16)
    for k in range(in_ref.shape[0]):
        out_ref[k] = total


def sum_call(pieces):
    return pl.pallas_call(
        sum_kernel,
        in_specs=[VMEM],
        out_specs=VMEM,
        out_shape=pltpu.VMEM(pieces.shape, BF16),
        compiler_params=pltpu.CompilerParams(vmem_limit_bytes=4 * 2**20),
        name="sum_pieces",
    )(on_chip(pieces))


def add_kernel(a_ref, b_ref, *out_refs):
    size = out_refs[0].shape[0]
    for k, out_ref in enumerate(out_refs):
        at = slice(k * size, (k + 1) * size)
        out_ref[...] = (a_ref[at, :].astype(F32) + b_ref[at, :].astype(F32)).astype(BF16)


def add_call(a, b, number):
    return pl.pallas_call(
        add_kernel,
        in_specs=[VMEM, VMEM],
        out_specs=[VMEM] * number,
        out_shape=[pltpu.VMEM((a.shape[0] // number, WIDTH), BF16)] * number,
        compiler_params=pltpu.CompilerParams(vmem_limit_bytes=4 * 2**20),
        name="add_cores",
    )(on_chip(a), on_chip(b))


def gather_kernel(own_ref, first_ref, *refs):
    *more, out_ref = refs
    core = lax.axis_index("dp") & 1
    total = jnp.where(core == 0, own_ref[...].astype(F32), first_ref[...].astype(F32))
    for ref in more:
        total += ref[...].astype(F32)
    out_ref[...] = total


def gather_call(own, pieces):
    return pl.pallas_call(
        gather_kernel,
        in_specs=[VMEM] * (1 + len(pieces)),
        out_specs=VMEM,
        out_shape=pltpu.VMEM(own.shape, F32),
        compiler_params=pltpu.CompilerParams(vmem_limit_bytes=4 * 2**20),
        name="sum_chips",
    )(on_chip(own), *[on_chip(p) for p in pieces])


def widen_kernel(other, first, picks, *refs):
    *parts, out_ref, wide_ref, sems = refs
    me = lax.axis_index("dp")
    core = (me & 1) ^ other
    block = parts[0].shape[0]
    copies = []
    for j, choice in enumerate(picks):
        if choice[0] == choice[1]:
            wide_ref[j] = parts[choice[0]][...].astype(F32)
        else:
            zero = parts[choice[0]][...].astype(F32)
            one = parts[choice[1]][...].astype(F32)
            wide_ref[j] = jnp.where(core == 0, zero, one)
        at = pl.ds(pl.multiple_of(owner(me, first + j, other) * block, block), block)
        copies.append(pltpu.make_async_copy(wide_ref.at[j], out_ref.at[at, :], sems.at[j]))
        copies[-1].start()
    for copy in copies:
        copy.wait()


def widen_call(parts, other, first, picks, base=None):
    block = parts[0].shape[0]
    more = [] if base is None else [base]
    count = len(parts)

    def kernel(*refs):
        widen_kernel(other, first, picks, *refs[:count], *refs[count + len(more) :])

    hbm = pl.BlockSpec(memory_space=pl.ANY)
    return pl.pallas_call(
        kernel,
        in_specs=[VMEM] * count + [hbm] * len(more),
        out_specs=hbm,
        out_shape=jax.ShapeDtypeStruct((8 * block, WIDTH), F32),
        input_output_aliases={count: 0} if more else {},
        scratch_shapes=[pltpu.VMEM((len(picks), block, WIDTH), F32), pltpu.SemaphoreType.DMA((len(picks),))],
        compiler_params=pltpu.CompilerParams(vmem_limit_bytes=4 * 2**20),
        name="widen",
    )(*[on_chip(p) for p in parts], *more)


def per_device(points, centers, direction):
    rows, count = points.shape[0], centers.shape[0]
    groups = lax.axis_size("center")
    swap = [(i, i ^ 1) for i in range(16)]

    tiles, partial_fit = fit_call(in_hbm(points), in_hbm(centers), in_hbm(direction))
    part = rows // groups
    pieces = lax.all_to_all(partial_fit.reshape(groups, part, WIDTH), "center", 0, 0)
    fitted = lax.all_to_all(sum_call(pieces), "center", 0, 0).reshape(rows, WIDTH)

    received = lax.ppermute(back_call(fitted, tiles, 1, 0, SETS), "dp", swap)
    sends = add_call(back_call(fitted, tiles, 0, 0, SETS), received, SETS)
    pieces = [exchange(sends[j], j) for j in range(SETS)]
    partial = gather_call(sends[0], pieces)
    (full,) = add_call(partial, lax.ppermute(partial, "dp", swap), 1)
    pieces = [exchange(full, j) for j in range(SETS)]
    others = [lax.ppermute(p, "dp", swap) for p in pieces]
    out = widen_call([full] + pieces, 0, 0, [(0, 1), (2, 2), (3, 3), (4, 4)])
    return widen_call([full] + others, 1, 0, [(0, 1), (2, 2), (3, 3), (4, 4)], out)


def solution(mesh):
    return jax.shard_map(
        per_device,
        mesh=mesh,
        in_specs=(P("dp", None), P("center", None), P("center", None)),
        out_specs=P("center", None),
        check_vma=False,
    )
```

time: 292 us -> 99.6 us (0.34)
  waiting for transfers between devices: 218 us -> 13.5 us
  matrix products: 49.1 us -> 0 us
  blocking collectives: 0 us -> 32.5 us
  starting transfers between devices: 0.04 us -> 27 us
  Pallas kernels: 0 us -> 26.2 us
  between operations: 13.4 us -> 0.12 us
  other arithmetic: 11.4 us -> 0 us
    psum x2 -> x0, waiting for transfers between devices: 218 us -> none  [the longest x1 133 us: per_device(): summed = lax.psum(partial_cols, 'dp')]
    dot_general x7 -> x0, matrix products: 49.1 us -> none  [the longest x3 26.4 us: kernel_tile(): cross = jnp.dot(pts, cens.T, preferred_element_type=jnp.float32)]
    all_to_all x0 -> x2, blocking collectives: none -> 32.5 us  [the longest x1 21.6 us: per_device(): lax.all_to_all(partial_fit.reshape(groups, part, WIDTH), 'center', 0, 0)]
    ppermute x0 -> x14, starting transfers between devices: none -> 27 us  [the longest x8 13.9 us: exchange(): return lax.ppermute(x, 'dp', pairs)]
    pallas_call x0 -> x9, Pallas kernels: none -> 26.2 us  [the longest x1 17.1 us: fit_call(): pl.pallas_call(functools.partial(fit_kernel, tile_rows), grid=(count // c...]
    ppermute x0 -> x14, waiting for transfers between devices: none -> 13.5 us  [the longest x8 11.7 us: exchange(): return lax.ppermute(x, 'dp', pairs)]
    div x1 -> x0, other arithmetic: 4.56 us -> none  [per_device(): return summed / jnp.sqrt(jnp.float32(total_points))]
    convert_element_type x2 -> x0, other arithmetic: 3.62 us -> none  [the longest x1 2.44 us: per_device(): dir_b = direction.astype(jnp.bfloat16)]
  transfers between devices with their start and end apart: 2 -> 14, of which waited for: 2 -> 6; matrix products, arithmetic and copies ran while one was open for 0% -> 0% of each run, Pallas kernels for 0% -> 4%
where the time goes in v2:
time: 99.6 us; the launch traced here: 99.4 us
  blocking collectives  32.5 us (33%)
  starting transfers between devices  27 us (27%)
  Pallas kernels  26.2 us (26%)
  waiting for transfers between devices  13.5 us (14%)
    all_to_all x1, blocking collectives, per_device(): lax.all_to_all(partial_fit.reshape(groups, part, WIDTH), 'center', 0, 0)  21.6 us
    pallas_call x1, Pallas kernels, fit_call(): pl.pallas_call(functools.partial(fit_kernel, tile_rows), grid=(count // c...  17.1 us
    ppermute x8, starting transfers between devices, exchange(): return lax.ppermute(x, 'dp', pairs)  13.9 us
    ppermute x8, waiting for transfers between devices, exchange(): return lax.ppermute(x, 'dp', pairs)  11.7 us
    all_to_all x1, blocking collectives, per_device(): lax.all_to_all(sum_call(pieces), 'center', 0, 0).reshape(rows, WIDTH)  10.9 us
    ppermute x4, starting transfers between devices, per_device(): others = [lax.ppermute(p, 'dp', swap) for p in pieces]  7.85 us
    pallas_call x2, Pallas kernels, back_call(): pl.pallas_call(functools.partial(back_kernel, other, first), grid=(number...  5.82 us
    ppermute x1, starting transfers between devices, per_device(): received = lax.ppermute(back_call(fitted, tiles, 1, 0, SETS), 'dp', swap)  3.09 us
  transfers between devices with their start and end apart: 14, of which 6 were waited for; matrix products, arithmetic and copies ran while one was open for 0% of the time, Pallas kernels for 4%

profile of v2, /device:TPU:1, one launch (start us, length us, event | category | flops | bytes accessed | tf_op | source)
XLA Modules:
  0.0 99.4 jit_solution(9009423675543290946)
XLA Ops:
  0.0 17.1 %fit_tiles.1 = (bf16[1536,8192]{1,0:T(8,128)(2,1)S(1)}, f32[1536,128]{1,0:T(8,128)S(1)}) custom-call(bf16[1536,128]{1,0:T(8,128)(2,1)} %points_ref.1, bf16[8192,128]{1,0:T(8,128)(2,1)} %centers_ref.1, f32[8192,128]{1,0:T(8,128)} %direction_ref.1), custom_call_target="tpu_custom_call" | custom-call | tf_op jit(solution)/shard_map/fit_tiles/pallas_call | solution.py:109
  17.1 21.6 %all_to_all.10.in_ref = f32[8,192,128]{2,1,0:T(8,128)S(1)} all-to-all(f32[8,192,128]{2,1,0:T(8,128)S(1)} %bitcast.4), channel_id=1, replica_groups=mesh['dp'=16,'center'=8] {'center'}, dimensions={0} | all-to-all | bytes 1572864 | tf_op jit(solution)/shard_map/all_to_all | solution.py:265
  38.7 10.9 %all_to_all.11 = bf16[8,192,128]{2,1,0:T(8,128)(2,1)S(1)} all-to-all(bf16[8,192,128]{2,1,0:T(8,128)(2,1)S(1)} %sum_pieces.1), channel_id=1, replica_groups=mesh['dp'=16,'center'=8] {'center'}, dimensions={0} | all-to-all | bytes 786432 | tf_op jit(solution)/shard_map/all_to_all | solution.py:266
  49.7 2.9 %back_tiles.3 = bf16[4096,128]{1,0:T(8,128)(2,1)S(1)} custom-call(bf16[1536,128]{1,0:T(8,128)(2,1)S(1)} %bitcast.2, bf16[1536,8192]{1,0:T(8,128)(2,1)S(1)} %get-tuple-element.12.tile_ref), custom_call_target="tpu_custom_call" | custom-call | tf_op jit(solution)/shard_map/back_tiles/pallas_call | solution.py:147
  52.6 3.1 %collective-permute-start = (bf16[4096,128]{1,0:T(8,128)(2,1)S(1)}, bf16[4096,128]{1,0:T(8,128)(2,1)S(1)}, u32[]{:S(2)}, u32[]{:S(2)}) collective-permute-start(bf16[4096,128]{1,0:T(8,128)(2,1)S(1)} %back_tiles.3), channel_id=1, source_target_pairs={{0,8},{8,0},{16,24},{24,16},{32,40},{40,32},{48,56},{56,48},{64,72... | collective-permute-start | bytes 3145736 | tf_op jit(solution)/shard_map/ppermute | solution.py:268
  55.7 2.9 %back_tiles.2.a_ref = bf16[4096,128]{1,0:T(8,128)(2,1)S(1)} custom-call(bf16[1536,128]{1,0:T(8,128)(2,1)S(1)} %bitcast.3, bf16[1536,8192]{1,0:T(8,128)(2,1)S(1)} %get-tuple-element.12.tile_ref), custom_call_target="tpu_custom_call" | custom-call | tf_op jit(solution)/shard_map/back_tiles/pallas_call | solution.py:147
  58.6 0.0 collective-permute-done.b_ref
  58.6 0.2 add_cores.2
  58.9 0.9 collective-permute-start.2
  59.7 1.6 %collective-permute-start.3 = (bf16[1024,128]{1,0:T(8,128)(2,1)S(1)}, bf16[1024,128]{1,0:T(8,128)(2,1)S(1)}, u32[]{:S(2)}, u32[]{:S(2)}) collective-permute-start(bf16[1024,128]{1,0:T(8,128)(2,1)S(1)} %get-tuple-element.15), channel_id=1, source_target_pairs={{0,80},{8,56},{16,64},{24,40},{32,112},{40,24},{48,96},{56,8},{64,... | collective-permute-start | bytes 786440 | tf_op jit(solution)/shard_map/ppermute | solution.py:52
  61.3 1.8 %collective-permute-start.4 = (bf16[1024,128]{1,0:T(8,128)(2,1)S(1)}, bf16[1024,128]{1,0:T(8,128)(2,1)S(1)}, u32[]{:S(2)}, u32[]{:S(2)}) collective-permute-start(bf16[1024,128]{1,0:T(8,128)(2,1)S(1)} %get-tuple-element.16), channel_id=1, source_target_pairs={{0,112},{8,104},{16,96},{24,120},{32,80},{40,72},{48,64},{56,88},{... | collective-permute-start | bytes 786440 | tf_op jit(solution)/shard_map/ppermute | solution.py:52
  63.1 2.5 %collective-permute-start.1 = (bf16[1024,128]{1,0:T(8,128)(2,1)S(1)}, bf16[1024,128]{1,0:T(8,128)(2,1)S(1)}, u32[]{:S(2)}, u32[]{:S(2)}) collective-permute-start(bf16[1024,128]{1,0:T(8,128)(2,1)S(1)} %get-tuple-element.13.own_ref), channel_id=1, source_target_pairs={{8,72},{24,88},{40,104},{56,120},{72,8},{88,24},{104,40},{120,56},... | collective-permute-start | bytes 786440 | tf_op jit(solution)/shard_map/ppermute | solution.py:52
  65.7 0.0 collective-permute-done.2.refs_0_
  65.7 2.9 %collective-permute-done.3.refs_1_ = bf16[1024,128]{1,0:T(8,128)(2,1)S(1)} collective-permute-done((bf16[1024,128]{1,0:T(8,128)(2,1)S(1)}, bf16[1024,128]{1,0:T(8,128)(2,1)S(1)}, u32[]{:S(2)}, u32[]{:S(2)}) %collective-permute-start.3) | collective-permute-done | bytes 262176 | tf_op jit(solution)/shard_map/ppermute | solution.py:52
  68.6 4.5 %collective-permute-done.4.refs_2_ = bf16[1024,128]{1,0:T(8,128)(2,1)S(1)} collective-permute-done((bf16[1024,128]{1,0:T(8,128)(2,1)S(1)}, bf16[1024,128]{1,0:T(8,128)(2,1)S(1)}, u32[]{:S(2)}, u32[]{:S(2)}) %collective-permute-start.4) | collective-permute-done | bytes 262176 | tf_op jit(solution)/shard_map/ppermute | solution.py:52
  73.1 2.5 %collective-permute-done.1.first_ref = bf16[1024,128]{1,0:T(8,128)(2,1)S(1)} collective-permute-done((bf16[1024,128]{1,0:T(8,128)(2,1)S(1)}, bf16[1024,128]{1,0:T(8,128)(2,1)S(1)}, u32[]{:S(2)}, u32[]{:S(2)}) %collective-permute-start.1) | collective-permute-done | bytes 262176 | tf_op jit(solution)/shard_map/ppermute | solution.py:52
  75.6 0.2 sum_chips.1.a_ref
  75.8 2.2 %collective-permute-start.5 = (f32[1024,128]{1,0:T(8,128)S(1)}, f32[1024,128]{1,0:T(8,128)S(1)}, u32[]{:S(2)}, u32[]{:S(2)}) collective-permute-start(f32[1024,128]{1,0:T(8,128)S(1)} %sum_chips.1.a_ref), channel_id=1, source_target_pairs={{0,8},{8,0},{16,24},{24,16},{32,40},{40,32},{48,56},{56,48},{64,72... | collective-permute-start | bytes 1572872 | tf_op jit(solution)/shard_map/ppermute | solution.py:272
  78.0 1.5 %collective-permute-done.5.b_ref = f32[1024,128]{1,0:T(8,128)S(1)} collective-permute-done((f32[1024,128]{1,0:T(8,128)S(1)}, f32[1024,128]{1,0:T(8,128)S(1)}, u32[]{:S(2)}, u32[]{:S(2)}) %collective-permute-start.5) | collective-permute-done | bytes 524320 | tf_op jit(solution)/shard_map/ppermute | solution.py:272
  79.6 1.5 %collective-permute-start.12 = (bf16[1024,128]{1,0:T(8,128)(2,1)S(1)}, bf16[1024,128]{1,0:T(8,128)(2,1)S(1)}, u32[]{:S(2)}, u32[]{:S(2)}) collective-permute-start(bf16[1024,128]{1,0:T(8,128)(2,1)S(1)} %add_cores.3.refs_0_), channel_id=1, source_target_pairs={{0,112},{8,104},{16,96},{24,120},{32,80},{40,72},{48,64},{56,88},{... | collective-permute-start | bytes 786440 | tf_op jit(solution)/shard_map/ppermute | solution.py:52
  81.1 0.0 collective-permute-start.10
  81.1 0.7 collective-permute-start.8
  81.8 4.8 %collective-permute-start.6 = (bf16[1024,128]{1,0:T(8,128)(2,1)S(1)}, bf16[1024,128]{1,0:T(8,128)(2,1)S(1)}, u32[]{:S(2)}, u32[]{:S(2)}) collective-permute-start(bf16[1024,128]{1,0:T(8,128)(2,1)S(1)} %add_cores.3.refs_0_), channel_id=1, source_target_pairs={{8,72},{24,88},{40,104},{56,120},{72,8},{88,24},{104,40},{120,56},... | collective-permute-start | bytes 786440 | tf_op jit(solution)/shard_map/ppermute | solution.py:52
  86.6 1.8 %collective-permute-done.12.refs_4_ = bf16[1024,128]{1,0:T(8,128)(2,1)S(1)} collective-permute-done((bf16[1024,128]{1,0:T(8,128)(2,1)S(1)}, bf16[1024,128]{1,0:T(8,128)(2,1)S(1)}, u32[]{:S(2)}, u32[]{:S(2)}) %collective-permute-start.12) | collective-permute-done | bytes 262176 | tf_op jit(solution)/shard_map/ppermute | solution.py:52
  88.4 7.3 %collective-permute-start.13 = (bf16[1024,128]{1,0:T(8,128)(2,1)S(1)}, bf16[1024,128]{1,0:T(8,128)(2,1)S(1)}, u32[]{:S(2)}, u32[]{:S(2)}) collective-permute-start(bf16[1024,128]{1,0:T(8,128)(2,1)S(1)} %collective-permute-done.12.refs_4_), channel_id=1, source_target_pairs={{0,8},{8,0},{16,24},{24,16},{32,40},{40,32},{48,56},{56,48},{64,72... | collective-permute-start | bytes 786440 | tf_op jit(solution)/shard_map/ppermute | solution.py:274
  95.7 0.0 collective-permute-done.10.refs_3_
  95.7 0.0 collective-permute-start.11
  95.7 0.0 collective-permute-done.8.refs_2_
  95.7 0.5 collective-permute-start.9
  96.2 0.0 collective-permute-done.6.refs_1_
  96.2 0.1 collective-permute-start.7
  96.3 1.4 %widen.2.refs_5_ = f32[8192,128]{1,0:T(8,128)} custom-call(bf16[1024,128]{1,0:T(8,128)(2,1)S(1)} %add_cores.3.refs_0_, bf16[1024,128]{1,0:T(8,128)(2,1)S(1)} %collective-permute-done.6.refs_1_, bf16[1024,128]{1,0:T(8,128)(2,1)S(1)} %collective-permute-done.8.refs_2_, bf16[1024,128]{1,0:T(8,128)(2,1)S(1)} %collective-permute-done.10.refs_3_, ...), custom_call_target="tpu_custom_call" | custom-call | tf_op jit(solution)/shard_map/widen/pallas_call | solution.py:246
  97.7 0.0 collective-permute-done.13.refs_4_
  97.7 0.0 collective-permute-done.11.refs_3_
  97.7 0.0 collective-permute-done.9.refs_2_
  97.7 0.2 collective-permute-done.7.refs_1_
  97.9 1.4 %widen.3 = f32[8192,128]{1,0:T(8,128)} custom-call(bf16[1024,128]{1,0:T(8,128)(2,1)S(1)} %add_cores.3.refs_0_, bf16[1024,128]{1,0:T(8,128)(2,1)S(1)} %collective-permute-done.7.refs_1_, bf16[1024,128]{1,0:T(8,128)(2,1)S(1)} %collective-permute-done.9.refs_2_, bf16[1024,128]{1,0:T(8,128)(2,1)S(1)} %collective-permute-done.11.refs_3_, ...), custom_call_target="tpu_custom_call", output_to_operand_aliasing={{}: (5, {})} | custom-call | tf_op jit(solution)/shard_map/widen/pallas_call | solution.py:246
  (2 shorter events, 0.1 us)
Async XLA Ops:
  52.6 6.0 %collective-permute-start = (bf16[4096,128]{1,0:T(8,128)(2,1)S(1)}, bf16[4096,128]{1,0:T(8,128)(2,1)S(1)}, u32[]{:S(2)}, u32[]{:S(2)}) collective-permute-start(bf16[4096,128]{1,0:T(8,128)(2,1)S(1)} %back_tiles.3), channel_id=1, source_target_pairs={{0,8},{8,0},{16,24},{24,16},{32,40},{40,32},{48,56},{56,48},{64,72... | collective-permute-start | bytes 3145736 | tf_op jit(solution)/shard_map/ppermute | solution.py:268
  58.9 6.9 %collective-permute-start.2 = (bf16[1024,128]{1,0:T(8,128)(2,1)S(1)}, bf16[1024,128]{1,0:T(8,128)(2,1)S(1)}, u32[]{:S(2)}, u32[]{:S(2)}) collective-permute-start(bf16[1024,128]{1,0:T(8,128)(2,1)S(1)} %get-tuple-element.14), channel_id=1, source_target_pairs={{0,32},{8,24},{16,48},{24,8},{32,0},{40,56},{48,16},{56,40},{64,96... | collective-permute-start | bytes 786440 | tf_op jit(solution)/shard_map/ppermute | solution.py:52
  59.7 8.9 %collective-permute-start.3 = (bf16[1024,128]{1,0:T(8,128)(2,1)S(1)}, bf16[1024,128]{1,0:T(8,128)(2,1)S(1)}, u32[]{:S(2)}, u32[]{:S(2)}) collective-permute-start(bf16[1024,128]{1,0:T(8,128)(2,1)S(1)} %get-tuple-element.15), channel_id=1, source_target_pairs={{0,80},{8,56},{16,64},{24,40},{32,112},{40,24},{48,96},{56,8},{64,... | collective-permute-start | bytes 786440 | tf_op jit(solution)/shard_map/ppermute | solution.py:52
  61.3 11.7 %collective-permute-start.4 = (bf16[1024,128]{1,0:T(8,128)(2,1)S(1)}, bf16[1024,128]{1,0:T(8,128)(2,1)S(1)}, u32[]{:S(2)}, u32[]{:S(2)}) collective-permute-start(bf16[1024,128]{1,0:T(8,128)(2,1)S(1)} %get-tuple-element.16), channel_id=1, source_target_pairs={{0,112},{8,104},{16,96},{24,120},{32,80},{40,72},{48,64},{56,88},{... | collective-permute-start | bytes 786440 | tf_op jit(solution)/shard_map/ppermute | solution.py:52
  63.1 12.5 %collective-permute-start.1 = (bf16[1024,128]{1,0:T(8,128)(2,1)S(1)}, bf16[1024,128]{1,0:T(8,128)(2,1)S(1)}, u32[]{:S(2)}, u32[]{:S(2)}) collective-permute-start(bf16[1024,128]{1,0:T(8,128)(2,1)S(1)} %get-tuple-element.13.own_ref), channel_id=1, source_target_pairs={{8,72},{24,88},{40,104},{56,120},{72,8},{88,24},{104,40},{120,56},... | collective-permute-start | bytes 786440 | tf_op jit(solution)/shard_map/ppermute | solution.py:52
  75.8 3.8 %collective-permute-start.5 = (f32[1024,128]{1,0:T(8,128)S(1)}, f32[1024,128]{1,0:T(8,128)S(1)}, u32[]{:S(2)}, u32[]{:S(2)}) collective-permute-start(f32[1024,128]{1,0:T(8,128)S(1)} %sum_chips.1.a_ref), channel_id=1, source_target_pairs={{0,8},{8,0},{16,24},{24,16},{32,40},{40,32},{48,56},{56,48},{64,72... | collective-permute-start | bytes 1572872 | tf_op jit(solution)/shard_map/ppermute | solution.py:272
  79.6 8.8 %collective-permute-start.12 = (bf16[1024,128]{1,0:T(8,128)(2,1)S(1)}, bf16[1024,128]{1,0:T(8,128)(2,1)S(1)}, u32[]{:S(2)}, u32[]{:S(2)}) collective-permute-start(bf16[1024,128]{1,0:T(8,128)(2,1)S(1)} %add_cores.3.refs_0_), channel_id=1, source_target_pairs={{0,112},{8,104},{16,96},{24,120},{32,80},{40,72},{48,64},{56,88},{... | collective-permute-start | bytes 786440 | tf_op jit(solution)/shard_map/ppermute | solution.py:52
  81.1 14.6 %collective-permute-start.10 = (bf16[1024,128]{1,0:T(8,128)(2,1)S(1)}, bf16[1024,128]{1,0:T(8,128)(2,1)S(1)}, u32[]{:S(2)}, u32[]{:S(2)}) collective-permute-start(bf16[1024,128]{1,0:T(8,128)(2,1)S(1)} %add_cores.3.refs_0_), channel_id=1, source_target_pairs={{0,80},{8,56},{16,64},{24,40},{32,112},{40,24},{48,96},{56,8},{64,... | collective-permute-start | bytes 786440 | tf_op jit(solution)/shard_map/ppermute | solution.py:52
  81.1 14.6 %collective-permute-start.8 = (bf16[1024,128]{1,0:T(8,128)(2,1)S(1)}, bf16[1024,128]{1,0:T(8,128)(2,1)S(1)}, u32[]{:S(2)}, u32[]{:S(2)}) collective-permute-start(bf16[1024,128]{1,0:T(8,128)(2,1)S(1)} %add_cores.3.refs_0_), channel_id=1, source_target_pairs={{0,32},{8,24},{16,48},{24,8},{32,0},{40,56},{48,16},{56,40},{64,96... | collective-permute-start | bytes 786440 | tf_op jit(solution)/shard_map/ppermute | solution.py:52
  81.8 14.4 %collective-permute-start.6 = (bf16[1024,128]{1,0:T(8,128)(2,1)S(1)}, bf16[1024,128]{1,0:T(8,128)(2,1)S(1)}, u32[]{:S(2)}, u32[]{:S(2)}) collective-permute-start(bf16[1024,128]{1,0:T(8,128)(2,1)S(1)} %add_cores.3.refs_0_), channel_id=1, source_target_pairs={{8,72},{24,88},{40,104},{56,120},{72,8},{88,24},{104,40},{120,56},... | collective-permute-start | bytes 786440 | tf_op jit(solution)/shard_map/ppermute | solution.py:52
  88.4 9.3 %collective-permute-start.13 = (bf16[1024,128]{1,0:T(8,128)(2,1)S(1)}, bf16[1024,128]{1,0:T(8,128)(2,1)S(1)}, u32[]{:S(2)}, u32[]{:S(2)}) collective-permute-start(bf16[1024,128]{1,0:T(8,128)(2,1)S(1)} %collective-permute-done.12.refs_4_), channel_id=1, source_target_pairs={{0,8},{8,0},{16,24},{24,16},{32,40},{40,32},{48,56},{56,48},{64,72... | collective-permute-start | bytes 786440 | tf_op jit(solution)/shard_map/ppermute | solution.py:274
  95.7 2.0 %collective-permute-start.11 = (bf16[1024,128]{1,0:T(8,128)(2,1)S(1)}, bf16[1024,128]{1,0:T(8,128)(2,1)S(1)}, u32[]{:S(2)}, u32[]{:S(2)}) collective-permute-start(bf16[1024,128]{1,0:T(8,128)(2,1)S(1)} %collective-permute-done.10.refs_3_), channel_id=1, source_target_pairs={{0,8},{8,0},{16,24},{24,16},{32,40},{40,32},{48,56},{56,48},{64,72... | collective-permute-start | bytes 786440 | tf_op jit(solution)/shard_map/ppermute | solution.py:274
  95.7 2.0 %collective-permute-start.9 = (bf16[1024,128]{1,0:T(8,128)(2,1)S(1)}, bf16[1024,128]{1,0:T(8,128)(2,1)S(1)}, u32[]{:S(2)}, u32[]{:S(2)}) collective-permute-start(bf16[1024,128]{1,0:T(8,128)(2,1)S(1)} %collective-permute-done.8.refs_2_), channel_id=1, source_target_pairs={{0,8},{8,0},{16,24},{24,16},{32,40},{40,32},{48,56},{56,48},{64,72... | collective-permute-start | bytes 786440 | tf_op jit(solution)/shard_map/ppermute | solution.py:274
  96.2 1.8 %collective-permute-start.7 = (bf16[1024,128]{1,0:T(8,128)(2,1)S(1)}, bf16[1024,128]{1,0:T(8,128)(2,1)S(1)}, u32[]{:S(2)}, u32[]{:S(2)}) collective-permute-start(bf16[1024,128]{1,0:T(8,128)(2,1)S(1)} %collective-permute-done.6.refs_1_), channel_id=1, source_target_pairs={{0,8},{8,0},{16,24},{24,16},{32,40},{40,32},{48,56},{56,48},{64,72... | collective-permute-start | bytes 786440 | tf_op jit(solution)/shard_map/ppermute | solution.py:274

commit v3 on v2

--- a/solution.py
+++ b/solution.py
@@ -32,7 +32,8 @@
 
 VMEM = pl.BlockSpec(memory_space=pltpu.VMEM)
 
-OFFSETS = ((0, 2, 5, 7), (4, 1, 3, 6))
+OFFSETS = ((4, 6, 1, 0), (5, 3, 7, 2))
+RELAY = (2, 6)
 SETS = len(OFFSETS[0])
 PACKED = [sum(k << (4 * j) for j, k in enumerate(row)) for row in OFFSETS]
 
@@ -42,13 +43,8 @@
     return (me >> 1) ^ ((table >> (4 * j)) & 7)
 
 
-def exchange(x, j):
-    pairs = [
-        (2 * chip + c, 2 * (chip ^ OFFSETS[c][j]) + c)
-        for chip in range(8)
-        for c in range(2)
-        if OFFSETS[c][j]
-    ]
+def exchange(x, hops):
+    pairs = [(2 * chip + c, 2 * (chip ^ hops[c]) + c) for chip in range(8) for c in range(2) if hops[c]]
     return lax.ppermute(x, "dp", pairs)
 
 
@@ -127,30 +123,25 @@
     )(points, centers, direction)
 
 
-def back_kernel(other, first, fitted_ref, tile_ref, out_ref, turned_ref):
-    step = pl.program_id(0)
-    cols = out_ref.shape[0] // pl.num_programs(0)
-
-    @pl.when(step == 0)
-    def _():
-        turned = fitted_ref[...].astype(F32).T * (1.0 / math.sqrt(POINTS))
-        turned_ref[...] = turned.astype(BF16)
-
-    piece = owner(lax.axis_index("dp"), first + step, other)
-    tile = tile_ref[:, pl.ds(pl.multiple_of(piece * cols, cols), cols)]
-    out = jnp.dot(turned_ref[...], tile, preferred_element_type=F32).T
-    out_ref[pl.ds(pl.multiple_of(step * cols, cols), cols), :] = out.astype(BF16)
-
-
-def back_call(fitted, tiles, other, first, number):
+def back_kernel(other, picks, fitted_ref, tile_ref, out_ref):
+    size = out_ref.shape[0] // len(picks)
+    me = lax.axis_index("dp")
+    turned = fitted_ref[...].astype(F32).T * (1.0 / math.sqrt(POINTS))
+    turned = turned.astype(BF16)
+    for n, j in enumerate(picks):
+        first = owner(me, j, other) * size
+        tile = tile_ref[:, pl.ds(pl.multiple_of(first, size), size)]
+        out = jnp.dot(turned, tile, preferred_element_type=F32).T
+        out_ref[n * size : (n + 1) * size, :] = out.astype(BF16)
+
+
+def back_call(fitted, tiles, other, picks):
     rows, count = tiles.shape
     return pl.pallas_call(
-        functools.partial(back_kernel, other, first),
-        grid=(number,),
+        functools.partial(back_kernel, other, picks),
         in_specs=[VMEM, VMEM],
         out_specs=VMEM,
-        out_shape=pltpu.VMEM((number * count // 8, WIDTH), BF16),
-        scratch_shapes=[pltpu.VMEM((WIDTH, rows), BF16)],
+        out_shape=pltpu.VMEM((len(picks) * count // 8, WIDTH), BF16),
         compiler_params=pltpu.CompilerParams(vmem_limit_bytes=30 * 2**20),
         name="back_tiles",
     )(on_chip(fitted), on_chip(tiles))
@@ -214,33 +205,32 @@
     )(on_chip(own), *[on_chip(p) for p in pieces])
 
 
-def widen_kernel(other, first, picks, *refs):
+def widen_kernel(picks, *refs):
     *parts, out_ref, wide_ref, sems = refs
     me = lax.axis_index("dp")
-    core = (me & 1) ^ other
     block = parts[0].shape[0]
     copies = []
-    for j, choice in enumerate(picks):
+    for n, (other, j, choice) in enumerate(picks):
         if choice[0] == choice[1]:
-            wide_ref[j] = parts[choice[0]][...].astype(F32)
+            wide_ref[n] = parts[choice[0]][...].astype(F32)
         else:
             zero = parts[choice[0]][...].astype(F32)
             one = parts[choice[1]][...].astype(F32)
-            wide_ref[j] = jnp.where(core == 0, zero, one)
-        at = pl.ds(pl.multiple_of(owner(me, first + j, other) * block, block), block)
-        copies.append(pltpu.make_async_copy(wide_ref.at[j], out_ref.at[at, :], sems.at[j]))
+            wide_ref[n] = jnp.where((me & 1) == other, zero, one)
+        at = pl.ds(pl.multiple_of(owner(me, j, other) * block, block), block)
+        copies.append(pltpu.make_async_copy(wide_ref.at[n], out_ref.at[at, :], sems.at[n]))
         copies[-1].start()
     for copy in copies:
         copy.wait()
 
 
-def widen_call(parts, other, first, picks, base=None):
+def widen_call(parts, picks, base=None):
     block = parts[0].shape[0]
     more = [] if base is None else [base]
     count = len(parts)
 
     def kernel(*refs):
-        widen_kernel(other, first, picks, *refs[:count], *refs[count + len(more) :])
+        widen_kernel(picks, *refs[:count], *refs[count + len(more) :])
 
     hbm = pl.BlockSpec(memory_space=pl.ANY)
     return pl.pallas_call(
@@ -265,15 +255,32 @@
     pieces = lax.all_to_all(partial_fit.reshape(groups, part, WIDTH), "center", 0, 0)
     fitted = lax.all_to_all(sum_call(pieces), "center", 0, 0).reshape(rows, WIDTH)
 
-    received = lax.ppermute(back_call(fitted, tiles, 1, 0, SETS), "dp", swap)
-    sends = add_call(back_call(fitted, tiles, 0, 0, SETS), received, SETS)
-    pieces = [exchange(sends[j], j) for j in range(SETS)]
-    partial = gather_call(sends[0], pieces)
+    sends = {}
+    halves = ((0, 2), (1, 3))
+    received = [lax.ppermute(back_call(fitted, tiles, 1, picks), "dp", swap) for picks in halves]
+    for picks, r in zip(halves, received):
+        sends.update(zip(picks, add_call(back_call(fitted, tiles, 0, picks), r, len(picks))))
+    hops = [tuple(row[j] for row in OFFSETS) for j in range(SETS)]
+    (relayed,) = add_call(sends[1], exchange(sends[0], RELAY), 1)
+    pieces = [exchange(x, h) for x, h in zip((sends[3], sends[2], relayed), hops[:0:-1])]
+    partial = gather_call(sends[3], pieces)
     (full,) = add_call(partial, lax.ppermute(partial, "dp", swap), 1)
-    pieces = [exchange(full, j) for j in range(SETS)]
-    others = [lax.ppermute(p, "dp", swap) for p in pieces]
-    out = widen_call([full] + pieces, 0, 0, [(0, 1), (2, 2), (3, 3), (4, 4)])
-    return widen_call([full] + others, 1, 0, [(0, 1), (2, 2), (3, 3), (4, 4)], out)
+    pieces = [exchange(full, h) for h in hops[1:]]
+    pieces = [exchange(pieces[0], RELAY)] + pieces
+    others = [None] + [lax.ppermute(p, "dp", swap) for p in pieces[1:]]
+
+    def write(out, *picks):
+        parts, chosen = [full], []
+        for other, j in picks:
+            parts.append((others if other else pieces)[j])
+            chosen.append((other, j, (0 if j == 3 else len(parts) - 1, len(parts) - 1)))
+        return widen_call(parts, chosen, out)
+
+    out = write(None, (0, 1), (0, 2), (0, 3), (1, 1))
+    pieces[0], out = lax.optimization_barrier((pieces[0], out))
+    others[0] = lax.ppermute(pieces[0], "dp", swap)
+    out = write(out, (1, 2), (1, 3), (0, 0))
+    return write(out, (1, 0))
 
 
 def solution(mesh):

time: 99.6 us -> 93.9 us (0.943)
  starting transfers between devices: 27 us -> 21.2 us
    ppermute x5 -> x6, starting transfers between devices: 10.9 us -> 7.86 us  [the longest x3 4.66 us: per_device(): others = [None] + [lax.ppermute(p, 'dp', swap) for p in pieces[1:]]]
    ppermute x1, starting transfers between devices: 2.22 us -> 0.33 us  [per_device(): full, = add_call(partial, lax.ppermute(partial, 'dp', swap), 1)]
    pallas_call x2 -> x4, Pallas kernels: 5.82 us -> 4.45 us  [back_call(): pl.pallas_call(functools.partial(back_kernel, other, picks), in_specs=[VM...]
    pallas_call x2 -> x3, Pallas kernels: 2.81 us -> 3.42 us  [widen_call(): pl.pallas_call(kernel, in_specs=[VMEM] * count + [hbm] * len(more), out_s...]
  transfers between devices with their start and end apart: 14 -> 15, of which waited for: 6 -> 7; matrix products, arithmetic and copies ran while one was open for 0% -> 0% of each run, Pallas kernels for 4% -> 7%
where the time goes in v3:
time: 93.9 us; the launch traced here: 93.7 us
  blocking collectives  32.5 us (35%)
  Pallas kernels  25.5 us (27%)
  starting transfers between devices  21.2 us (23%)
  waiting for transfers between devices  14.3 us (15%)
    all_to_all x1, blocking collectives, per_device(): lax.all_to_all(partial_fit.reshape(groups, part, WIDTH), 'center', 0, 0)  21.6 us
    pallas_call x1, Pallas kernels, fit_call(): pl.pallas_call(functools.partial(fit_kernel, tile_rows), grid=(count // c...  17.1 us
    ppermute x8, starting transfers between devices, exchange(): return lax.ppermute(x, 'dp', pairs)  13 us
    ppermute x8, waiting for transfers between devices, exchange(): return lax.ppermute(x, 'dp', pairs)  12.3 us
    all_to_all x1, blocking collectives, per_device(): lax.all_to_all(sum_call(pieces), 'center', 0, 0).reshape(rows, WIDTH)  10.9 us
    ppermute x3, starting transfers between devices, per_device(): others = [None] + [lax.ppermute(p, 'dp', swap) for p in pieces[1:]]  4.66 us
    pallas_call x4, Pallas kernels, back_call(): pl.pallas_call(functools.partial(back_kernel, other, picks), in_specs=[VM...  4.45 us
    pallas_call x3, Pallas kernels, widen_call(): pl.pallas_call(kernel, in_specs=[VMEM] * count + [hbm] * len(more), out_s...  3.42 us
  transfers between devices with their start and end apart: 15, of which 7 were waited for; matrix products, arithmetic and copies ran while one was open for 0% of the time, Pallas kernels for 7%

profile of v3, /device:TPU:1, one launch (start us, length us, event | category | flops | bytes accessed | tf_op | source)
XLA Modules:
  0.0 93.7 jit_solution(10063075248687023893)
XLA Ops:
  0.0 17.1 %fit_tiles.1 = (bf16[1536,8192]{1,0:T(8,128)(2,1)S(1)}, f32[1536,128]{1,0:T(8,128)S(1)}) custom-call(bf16[1536,128]{1,0:T(8,128)(2,1)} %points_ref.1, bf16[8192,128]{1,0:T(8,128)(2,1)} %centers_ref.1, f32[8192,128]{1,0:T(8,128)} %direction_ref.1), custom_call_target="tpu_custom_call" | custom-call | tf_op jit(solution)/shard_map/fit_tiles/pallas_call | solution.py:105
  17.1 21.6 %all_to_all.10.in_ref = f32[8,192,128]{2,1,0:T(8,128)S(1)} all-to-all(f32[8,192,128]{2,1,0:T(8,128)S(1)} %bitcast.6), channel_id=1, replica_groups=mesh['dp'=16,'center'=8] {'center'}, dimensions={0} | all-to-all | bytes 1572864 | tf_op jit(solution)/shard_map/all_to_all | solution.py:255
  38.7 10.9 %all_to_all.11 = bf16[8,192,128]{2,1,0:T(8,128)(2,1)S(1)} all-to-all(bf16[8,192,128]{2,1,0:T(8,128)(2,1)S(1)} %sum_pieces.1), channel_id=1, replica_groups=mesh['dp'=16,'center'=8] {'center'}, dimensions={0} | all-to-all | bytes 786432 | tf_op jit(solution)/shard_map/all_to_all | solution.py:256
  49.7 1.1 %back_tiles.7 = bf16[2048,128]{1,0:T(8,128)(2,1)S(1)} custom-call(bf16[1536,128]{1,0:T(8,128)(2,1)S(1)} %bitcast.2, bf16[1536,8192]{1,0:T(8,128)(2,1)S(1)} %get-tuple-element.14.tile_ref), custom_call_target="tpu_custom_call" | custom-call | tf_op jit(solution)/shard_map/back_tiles/pallas_call | solution.py:140
  50.8 3.1 %collective-permute-start.2 = (bf16[2048,128]{1,0:T(8,128)(2,1)S(1)}, bf16[2048,128]{1,0:T(8,128)(2,1)S(1)}, u32[]{:S(2)}, u32[]{:S(2)}) collective-permute-start(bf16[2048,128]{1,0:T(8,128)(2,1)S(1)} %back_tiles.7), channel_id=1, source_target_pairs={{0,8},{8,0},{16,24},{24,16},{32,40},{40,32},{48,56},{56,48},{64,72... | collective-permute-start | bytes 1572872 | tf_op jit(solution)/shard_map/ppermute | solution.py:260
  53.9 1.1 %back_tiles.5 = bf16[2048,128]{1,0:T(8,128)(2,1)S(1)} custom-call(bf16[1536,128]{1,0:T(8,128)(2,1)S(1)} %bitcast.3, bf16[1536,8192]{1,0:T(8,128)(2,1)S(1)} %get-tuple-element.14.tile_ref), custom_call_target="tpu_custom_call" | custom-call | tf_op jit(solution)/shard_map/back_tiles/pallas_call | solution.py:140
  55.0 0.1 collective-permute-start
  55.1 1.1 %back_tiles.6.a_ref = bf16[2048,128]{1,0:T(8,128)(2,1)S(1)} custom-call(bf16[1536,128]{1,0:T(8,128)(2,1)S(1)} %bitcast.4, bf16[1536,8192]{1,0:T(8,128)(2,1)S(1)} %get-tuple-element.14.tile_ref), custom_call_target="tpu_custom_call" | custom-call | tf_op jit(solution)/shard_map/back_tiles/pallas_call | solution.py:140
  56.2 0.0 collective-permute-done.2.b_ref
  56.2 0.1 add_cores.5
  56.4 2.6 %collective-permute-start.4 = (bf16[1024,128]{1,0:T(8,128)(2,1)S(1)}, bf16[1024,128]{1,0:T(8,128)(2,1)S(1)}, u32[]{:S(2)}, u32[]{:S(2)}) collective-permute-start(bf16[1024,128]{1,0:T(8,128)(2,1)S(1)} %get-tuple-element.18), channel_id=1, source_target_pairs={{0,32},{8,104},{16,48},{24,120},{32,0},{40,72},{48,16},{56,88},{64... | collective-permute-start | bytes 786440 | tf_op jit(solution)/shard_map/ppermute | solution.py:48
  58.9 1.1 %back_tiles.4.a_ref = bf16[2048,128]{1,0:T(8,128)(2,1)S(1)} custom-call(bf16[1536,128]{1,0:T(8,128)(2,1)S(1)} %bitcast.5, bf16[1536,8192]{1,0:T(8,128)(2,1)S(1)} %get-tuple-element.14.tile_ref), custom_call_target="tpu_custom_call" | custom-call | tf_op jit(solution)/shard_map/back_tiles/pallas_call | solution.py:140
  60.0 0.0 collective-permute-done.b_ref
  60.0 0.1 add_cores.4
  60.2 1.9 %collective-permute-start.1 = (bf16[1024,128]{1,0:T(8,128)(2,1)S(1)}, bf16[1024,128]{1,0:T(8,128)(2,1)S(1)}, u32[]{:S(2)}, u32[]{:S(2)}) collective-permute-start(bf16[1024,128]{1,0:T(8,128)(2,1)S(1)} %get-tuple-element.15.own_ref), channel_id=1, source_target_pairs={{8,40},{24,56},{40,8},{56,24},{72,104},{88,120},{104,72},{120,88},... | collective-permute-start | bytes 786440 | tf_op jit(solution)/shard_map/ppermute | solution.py:48
  62.1 1.3 %collective-permute-start.3 = (bf16[1024,128]{1,0:T(8,128)(2,1)S(1)}, bf16[1024,128]{1,0:T(8,128)(2,1)S(1)}, u32[]{:S(2)}, u32[]{:S(2)}) collective-permute-start(bf16[1024,128]{1,0:T(8,128)(2,1)S(1)} %get-tuple-element.16), channel_id=1, source_target_pairs={{0,16},{8,120},{16,0},{24,104},{32,48},{40,88},{48,32},{56,72},{64... | collective-permute-start | bytes 786440 | tf_op jit(solution)/shard_map/ppermute | solution.py:48
  63.4 0.0 collective-permute-done.4.b_ref
  63.4 0.1 add_cores.6
  63.5 0.8 collective-permute-start.5
  64.3 3.0 %collective-permute-done.1.first_ref = bf16[1024,128]{1,0:T(8,128)(2,1)S(1)} collective-permute-done((bf16[1024,128]{1,0:T(8,128)(2,1)S(1)}, bf16[1024,128]{1,0:T(8,128)(2,1)S(1)}, u32[]{:S(2)}, u32[]{:S(2)}) %collective-permute-start.1) | collective-permute-done | bytes 262176 | tf_op jit(solution)/shard_map/ppermute | solution.py:48
  67.3 4.6 %collective-permute-done.3.refs_0_ = bf16[1024,128]{1,0:T(8,128)(2,1)S(1)} collective-permute-done((bf16[1024,128]{1,0:T(8,128)(2,1)S(1)}, bf16[1024,128]{1,0:T(8,128)(2,1)S(1)}, u32[]{:S(2)}, u32[]{:S(2)}) %collective-permute-start.3) | collective-permute-done | bytes 262176 | tf_op jit(solution)/shard_map/ppermute | solution.py:48
  71.9 0.5 collective-permute-done.5.refs_1_
  72.3 0.1 sum_chips.1.a_ref
  72.5 0.3 collective-permute-start.6
  72.8 1.7 %collective-permute-done.6.b_ref = f32[1024,128]{1,0:T(8,128)S(1)} collective-permute-done((f32[1024,128]{1,0:T(8,128)S(1)}, f32[1024,128]{1,0:T(8,128)S(1)}, u32[]{:S(2)}, u32[]{:S(2)}) %collective-permute-start.6) | collective-permute-done | bytes 524320 | tf_op jit(solution)/shard_map/ppermute | solution.py:267
  74.5 0.8 collective-permute-start.7
  75.3 2.7 %collective-permute-start.9 = (bf16[1024,128]{1,0:T(8,128)(2,1)S(1)}, bf16[1024,128]{1,0:T(8,128)(2,1)S(1)}, u32[]{:S(2)}, u32[]{:S(2)}) collective-permute-start(bf16[1024,128]{1,0:T(8,128)(2,1)S(1)} %add_cores.7.refs_0_), channel_id=1, source_target_pairs={{0,16},{8,120},{16,0},{24,104},{32,48},{40,88},{48,32},{56,72},{64... | collective-permute-start | bytes 786440 | tf_op jit(solution)/shard_map/ppermute | solution.py:48
  78.0 1.9 %collective-permute-start.10 = (bf16[1024,128]{1,0:T(8,128)(2,1)S(1)}, bf16[1024,128]{1,0:T(8,128)(2,1)S(1)}, u32[]{:S(2)}, u32[]{:S(2)}) collective-permute-start(bf16[1024,128]{1,0:T(8,128)(2,1)S(1)} %add_cores.7.refs_0_), channel_id=1, source_target_pairs={{8,40},{24,56},{40,8},{56,24},{72,104},{88,120},{104,72},{120,88},... | collective-permute-start | bytes 786440 | tf_op jit(solution)/shard_map/ppermute | solution.py:48
  79.9 1.4 %collective-permute-done.7.refs_1_ = bf16[1024,128]{1,0:T(8,128)(2,1)S(1)} collective-permute-done((bf16[1024,128]{1,0:T(8,128)(2,1)S(1)}, bf16[1024,128]{1,0:T(8,128)(2,1)S(1)}, u32[]{:S(2)}, u32[]{:S(2)}) %collective-permute-start.7) | collective-permute-done | bytes 262176 | tf_op jit(solution)/shard_map/ppermute | solution.py:48
  81.3 3.6 %collective-permute-start.11 = (bf16[1024,128]{1,0:T(8,128)(2,1)S(1)}, bf16[1024,128]{1,0:T(8,128)(2,1)S(1)}, u32[]{:S(2)}, u32[]{:S(2)}) collective-permute-start(bf16[1024,128]{1,0:T(8,128)(2,1)S(1)} %collective-permute-done.7.refs_1_), channel_id=1, source_target_pairs={{0,8},{8,0},{16,24},{24,16},{32,40},{40,32},{48,56},{56,48},{64,72... | collective-permute-start | bytes 786440 | tf_op jit(solution)/shard_map/ppermute | solution.py:270
  84.9 1.1 %collective-permute-start.8 = (bf16[1024,128]{1,0:T(8,128)(2,1)S(1)}, bf16[1024,128]{1,0:T(8,128)(2,1)S(1)}, u32[]{:S(2)}, u32[]{:S(2)}) collective-permute-start(bf16[1024,128]{1,0:T(8,128)(2,1)S(1)} %collective-permute-done.7.refs_1_), channel_id=1, source_target_pairs={{0,32},{8,104},{16,48},{24,120},{32,0},{40,72},{48,16},{56,88},{64... | collective-permute-start | bytes 786440 | tf_op jit(solution)/shard_map/ppermute | solution.py:48
  85.9 0.0 collective-permute-done.9.refs_2_
  85.9 1.1 %collective-permute-start.13 = (bf16[1024,128]{1,0:T(8,128)(2,1)S(1)}, bf16[1024,128]{1,0:T(8,128)(2,1)S(1)}, u32[]{:S(2)}, u32[]{:S(2)}) collective-permute-start(bf16[1024,128]{1,0:T(8,128)(2,1)S(1)} %collective-permute-done.9.refs_2_), channel_id=1, source_target_pairs={{0,8},{8,0},{16,24},{24,16},{32,40},{40,32},{48,56},{56,48},{64,72... | collective-permute-start | bytes 786440 | tf_op jit(solution)/shard_map/ppermute | solution.py:270
  87.0 0.0 collective-permute-done.10.refs_3_
  87.0 0.0 collective-permute-start.14
  87.0 0.0 collective-permute-done.11.refs_4_
  87.0 1.4 %widen.3.refs_4_ = f32[8192,128]{1,0:T(8,128)} custom-call(bf16[1024,128]{1,0:T(8,128)(2,1)S(1)} %add_cores.7.refs_0_, bf16[1024,128]{1,0:T(8,128)(2,1)S(1)} %collective-permute-done.7.refs_1_, bf16[1024,128]{1,0:T(8,128)(2,1)S(1)} %collective-permute-done.9.refs_2_, bf16[1024,128]{1,0:T(8,128)(2,1)S(1)} %collective-permute-done.10.refs_3_, ...), custom_call_target="tpu_custom_call" | custom-call | tf_op jit(solution)/shard_map/widen/pallas_call | solution.py:236
  88.4 2.9 %collective-permute-done.8.refs_3_ = bf16[1024,128]{1,0:T(8,128)(2,1)S(1)} collective-permute-done((bf16[1024,128]{1,0:T(8,128)(2,1)S(1)}, bf16[1024,128]{1,0:T(8,128)(2,1)S(1)}, u32[]{:S(2)}, u32[]{:S(2)}) %collective-permute-start.8) | collective-permute-done | bytes 262176 | tf_op jit(solution)/shard_map/ppermute | solution.py:48
  91.3 0.0 collective-permute-start.12
  91.3 0.0 collective-permute-done.13.refs_1_
  91.3 0.0 collective-permute-done.14.refs_2_
  91.3 1.2 %widen.4.refs_2_ = f32[8192,128]{1,0:T(8,128)} custom-call(bf16[1024,128]{1,0:T(8,128)(2,1)S(1)} %add_cores.7.refs_0_, bf16[1024,128]{1,0:T(8,128)(2,1)S(1)} %collective-permute-done.13.refs_1_, bf16[1024,128]{1,0:T(8,128)(2,1)S(1)} %collective-permute-done.14.refs_2_, ...), custom_call_target="tpu_custom_call", output_to_operand_aliasing={{}: (4, {})} | custom-call | tf_op jit(solution)/shard_map/widen/pallas_call | solution.py:236
  92.5 0.3 collective-permute-done.12.refs_1_
  92.8 0.8 widen.5
  (2 shorter events, 0.1 us)
Async XLA Ops:
  50.8 5.4 %collective-permute-start.2 = (bf16[2048,128]{1,0:T(8,128)(2,1)S(1)}, bf16[2048,128]{1,0:T(8,128)(2,1)S(1)}, u32[]{:S(2)}, u32[]{:S(2)}) collective-permute-start(bf16[2048,128]{1,0:T(8,128)(2,1)S(1)} %back_tiles.7), channel_id=1, source_target_pairs={{0,8},{8,0},{16,24},{24,16},{32,40},{40,32},{48,56},{56,48},{64,72... | collective-permute-start | bytes 1572872 | tf_op jit(solution)/shard_map/ppermute | solution.py:260
  55.0 5.0 %collective-permute-start = (bf16[2048,128]{1,0:T(8,128)(2,1)S(1)}, bf16[2048,128]{1,0:T(8,128)(2,1)S(1)}, u32[]{:S(2)}, u32[]{:S(2)}) collective-permute-start(bf16[2048,128]{1,0:T(8,128)(2,1)S(1)} %back_tiles.5), channel_id=1, source_target_pairs={{0,8},{8,0},{16,24},{24,16},{32,40},{40,32},{48,56},{56,48},{64,72... | collective-permute-start | bytes 1572872 | tf_op jit(solution)/shard_map/ppermute | solution.py:260
  56.4 7.1 %collective-permute-start.4 = (bf16[1024,128]{1,0:T(8,128)(2,1)S(1)}, bf16[1024,128]{1,0:T(8,128)(2,1)S(1)}, u32[]{:S(2)}, u32[]{:S(2)}) collective-permute-start(bf16[1024,128]{1,0:T(8,128)(2,1)S(1)} %get-tuple-element.18), channel_id=1, source_target_pairs={{0,32},{8,104},{16,48},{24,120},{32,0},{40,72},{48,16},{56,88},{64... | collective-permute-start | bytes 786440 | tf_op jit(solution)/shard_map/ppermute | solution.py:48
  60.2 7.1 %collective-permute-start.1 = (bf16[1024,128]{1,0:T(8,128)(2,1)S(1)}, bf16[1024,128]{1,0:T(8,128)(2,1)S(1)}, u32[]{:S(2)}, u32[]{:S(2)}) collective-permute-start(bf16[1024,128]{1,0:T(8,128)(2,1)S(1)} %get-tuple-element.15.own_ref), channel_id=1, source_target_pairs={{8,40},{24,56},{40,8},{56,24},{72,104},{88,120},{104,72},{120,88},... | collective-permute-start | bytes 786440 | tf_op jit(solution)/shard_map/ppermute | solution.py:48
  62.1 9.7 %collective-permute-start.3 = (bf16[1024,128]{1,0:T(8,128)(2,1)S(1)}, bf16[1024,128]{1,0:T(8,128)(2,1)S(1)}, u32[]{:S(2)}, u32[]{:S(2)}) collective-permute-start(bf16[1024,128]{1,0:T(8,128)(2,1)S(1)} %get-tuple-element.16), channel_id=1, source_target_pairs={{0,16},{8,120},{16,0},{24,104},{32,48},{40,88},{48,32},{56,72},{64... | collective-permute-start | bytes 786440 | tf_op jit(solution)/shard_map/ppermute | solution.py:48
  63.5 8.8 %collective-permute-start.5 = (bf16[1024,128]{1,0:T(8,128)(2,1)S(1)}, bf16[1024,128]{1,0:T(8,128)(2,1)S(1)}, u32[]{:S(2)}, u32[]{:S(2)}) collective-permute-start(bf16[1024,128]{1,0:T(8,128)(2,1)S(1)} %add_cores.6), channel_id=1, source_target_pairs={{0,96},{8,56},{16,112},{24,40},{32,64},{40,24},{48,80},{56,8},{64,... | collective-permute-start | bytes 786440 | tf_op jit(solution)/shard_map/ppermute | solution.py:48
  72.5 2.0 %collective-permute-start.6 = (f32[1024,128]{1,0:T(8,128)S(1)}, f32[1024,128]{1,0:T(8,128)S(1)}, u32[]{:S(2)}, u32[]{:S(2)}) collective-permute-start(f32[1024,128]{1,0:T(8,128)S(1)} %sum_chips.1.a_ref), channel_id=1, source_target_pairs={{0,8},{8,0},{16,24},{24,16},{32,40},{40,32},{48,56},{56,48},{64,72... | collective-permute-start | bytes 1572872 | tf_op jit(solution)/shard_map/ppermute | solution.py:267
  74.5 6.8 %collective-permute-start.7 = (bf16[1024,128]{1,0:T(8,128)(2,1)S(1)}, bf16[1024,128]{1,0:T(8,128)(2,1)S(1)}, u32[]{:S(2)}, u32[]{:S(2)}) collective-permute-start(bf16[1024,128]{1,0:T(8,128)(2,1)S(1)} %add_cores.7.refs_0_), channel_id=1, source_target_pairs={{0,96},{8,56},{16,112},{24,40},{32,64},{40,24},{48,80},{56,8},{64,... | collective-permute-start | bytes 786440 | tf_op jit(solution)/shard_map/ppermute | solution.py:48
  75.3 10.6 %collective-permute-start.9 = (bf16[1024,128]{1,0:T(8,128)(2,1)S(1)}, bf16[1024,128]{1,0:T(8,128)(2,1)S(1)}, u32[]{:S(2)}, u32[]{:S(2)}) collective-permute-start(bf16[1024,128]{1,0:T(8,128)(2,1)S(1)} %add_cores.7.refs_0_), channel_id=1, source_target_pairs={{0,16},{8,120},{16,0},{24,104},{32,48},{40,88},{48,32},{56,72},{64... | collective-permute-start | bytes 786440 | tf_op jit(solution)/shard_map/ppermute | solution.py:48
  78.0 9.1 %collective-permute-start.10 = (bf16[1024,128]{1,0:T(8,128)(2,1)S(1)}, bf16[1024,128]{1,0:T(8,128)(2,1)S(1)}, u32[]{:S(2)}, u32[]{:S(2)}) collective-permute-start(bf16[1024,128]{1,0:T(8,128)(2,1)S(1)} %add_cores.7.refs_0_), channel_id=1, source_target_pairs={{8,40},{24,56},{40,8},{56,24},{72,104},{88,120},{104,72},{120,88},... | collective-permute-start | bytes 786440 | tf_op jit(solution)/shard_map/ppermute | solution.py:48
  81.3 5.7 %collective-permute-start.11 = (bf16[1024,128]{1,0:T(8,128)(2,1)S(1)}, bf16[1024,128]{1,0:T(8,128)(2,1)S(1)}, u32[]{:S(2)}, u32[]{:S(2)}) collective-permute-start(bf16[1024,128]{1,0:T(8,128)(2,1)S(1)} %collective-permute-done.7.refs_1_), channel_id=1, source_target_pairs={{0,8},{8,0},{16,24},{24,16},{32,40},{40,32},{48,56},{56,48},{64,72... | collective-permute-start | bytes 786440 | tf_op jit(solution)/shard_map/ppermute | solution.py:270
  84.9 6.4 %collective-permute-start.8 = (bf16[1024,128]{1,0:T(8,128)(2,1)S(1)}, bf16[1024,128]{1,0:T(8,128)(2,1)S(1)}, u32[]{:S(2)}, u32[]{:S(2)}) collective-permute-start(bf16[1024,128]{1,0:T(8,128)(2,1)S(1)} %collective-permute-done.7.refs_1_), channel_id=1, source_target_pairs={{0,32},{8,104},{16,48},{24,120},{32,0},{40,72},{48,16},{56,88},{64... | collective-permute-start | bytes 786440 | tf_op jit(solution)/shard_map/ppermute | solution.py:48
  85.9 5.4 %collective-permute-start.13 = (bf16[1024,128]{1,0:T(8,128)(2,1)S(1)}, bf16[1024,128]{1,0:T(8,128)(2,1)S(1)}, u32[]{:S(2)}, u32[]{:S(2)}) collective-permute-start(bf16[1024,128]{1,0:T(8,128)(2,1)S(1)} %collective-permute-done.9.refs_2_), channel_id=1, source_target_pairs={{0,8},{8,0},{16,24},{24,16},{32,40},{40,32},{48,56},{56,48},{64,72... | collective-permute-start | bytes 786440 | tf_op jit(solution)/shard_map/ppermute | solution.py:270
  87.0 4.3 %collective-permute-start.14 = (bf16[1024,128]{1,0:T(8,128)(2,1)S(1)}, bf16[1024,128]{1,0:T(8,128)(2,1)S(1)}, u32[]{:S(2)}, u32[]{:S(2)}) collective-permute-start(bf16[1024,128]{1,0:T(8,128)(2,1)S(1)} %collective-permute-done.10.refs_3_), channel_id=1, source_target_pairs={{0,8},{8,0},{16,24},{24,16},{32,40},{40,32},{48,56},{56,48},{64,72... | collective-permute-start | bytes 786440 | tf_op jit(solution)/shard_map/ppermute | solution.py:270
  91.3 1.5 %collective-permute-start.12 = (bf16[1024,128]{1,0:T(8,128)(2,1)S(1)}, bf16[1024,128]{1,0:T(8,128)(2,1)S(1)}, u32[]{:S(2)}, u32[]{:S(2)}) collective-permute-start(bf16[1024,128]{1,0:T(8,128)(2,1)S(1)} %collective-permute-done.8.refs_3_), channel_id=1, source_target_pairs={{0,8},{8,0},{16,24},{24,16},{32,40},{40,32},{48,56},{56,48},{64,72... | collective-permute-start | bytes 786440 | tf_op jit(solution)/shard_map/ppermute | solution.py:281

commit v4 on v3

--- a/solution.py
+++ b/solution.py
@@ -87,12 +87,12 @@
         sum_ref[at, :] += jnp.dot(tile, weights_ref[...], preferred_element_type=F32)
 
     count = rows // tile_rows
-    last = make(0)
-    for t in range(1, count):
-        tile = make(t)
-        fit(t - 1, last)
-        last = tile
-    fit(count - 1, last)
+    made = []
+    for t in range(count + 2):
+        if t < count:
+            made.append(make(t))
+        if t >= 2:
+            fit(t - 2, made[t - 2])
 
     @pl.when(step == pl.num_programs(0) - 1)
     def _():
@@ -123,8 +123,10 @@
     )(points, centers, direction)
 
 
-def back_kernel(other, picks, fitted_ref, tile_ref, out_ref):
-    size = out_ref.shape[0] // len(picks)
+def back_kernel(other, picks, fitted_ref, tile_ref, *refs):
+    *received, first_ref = refs[: len(refs) - (1 if other else len(picks)) + 1]
+    out_refs = refs[len(received) :]
+    size = first_ref.shape[0] // (len(picks) if other else 1)
     me = lax.axis_index("dp")
     turned = fitted_ref[...].astype(F32).T * (1.0 / math.sqrt(POINTS))
     turned = turned.astype(BF16)
@@ -132,19 +134,24 @@
         first = owner(me, j, other) * size
         tile = tile_ref[:, pl.ds(pl.multiple_of(first, size), size)]
         out = jnp.dot(turned, tile, preferred_element_type=F32).T
-        out_ref[n * size : (n + 1) * size, :] = out.astype(BF16)
-
-
-def back_call(fitted, tiles, other, picks):
+        at = slice(n * size, (n + 1) * size)
+        if other:
+            first_ref[at, :] = out.astype(BF16)
+        else:
+            out_refs[n][...] = (out + received[0][at, :].astype(F32)).astype(BF16)
+
+
+def back_call(fitted, tiles, other, picks, *received):
     rows, count = tiles.shape
+    each = 1 if other else len(picks)
     return pl.pallas_call(
         functools.partial(back_kernel, other, picks),
-        in_specs=[VMEM, VMEM],
-        out_specs=VMEM,
-        out_shape=pltpu.VMEM((len(picks) * count // 8, WIDTH), BF16),
+        in_specs=[VMEM] * (2 + len(received)),
+        out_specs=[VMEM] * each,
+        out_shape=[pltpu.VMEM((len(picks) * count // 8 // each, WIDTH), BF16)] * each,
         compiler_params=pltpu.CompilerParams(vmem_limit_bytes=30 * 2**20),
         name="back_tiles",
-    )(on_chip(fitted), on_chip(tiles))
+    )(on_chip(fitted), on_chip(tiles), *[on_chip(r) for r in received])
 
 
 def sum_kernel(in_ref, out_ref):
@@ -167,42 +174,39 @@
     )(on_chip(pieces))
 
 
-def add_kernel(a_ref, b_ref, *out_refs):
-    size = out_refs[0].shape[0]
-    for k, out_ref in enumerate(out_refs):
-        at = slice(k * size, (k + 1) * size)
-        out_ref[...] = (a_ref[at, :].astype(F32) + b_ref[at, :].astype(F32)).astype(BF16)
-
-
-def add_call(a, b, number):
+def add_kernel(a_ref, b_ref, out_ref):
+    out_ref[...] = (a_ref[...].astype(F32) + b_ref[...].astype(F32)).astype(BF16)
+
+
+def add_call(a, b):
     return pl.pallas_call(
         add_kernel,
         in_specs=[VMEM, VMEM],
-        out_specs=[VMEM] * number,
-        out_shape=[pltpu.VMEM((a.shape[0] // number, WIDTH), BF16)] * number,
+        out_specs=VMEM,
+        out_shape=pltpu.VMEM(a.shape, BF16),
         compiler_params=pltpu.CompilerParams(vmem_limit_bytes=4 * 2**20),
-        name="add_cores",
+        name="add_pieces",
     )(on_chip(a), on_chip(b))
 
 
-def gather_kernel(own_ref, first_ref, *refs):
-    *more, out_ref = refs
-    core = lax.axis_index("dp") & 1
-    total = jnp.where(core == 0, own_ref[...].astype(F32), first_ref[...].astype(F32))
-    for ref in more:
-        total += ref[...].astype(F32)
-    out_ref[...] = total
-
-
-def gather_call(own, pieces):
-    return pl.pallas_call(
-        gather_kernel,
-        in_specs=[VMEM] * (1 + len(pieces)),
+def begin_kernel(own_ref, along_ref, out_ref):
+    own = jnp.where((lax.axis_index("dp") & 1) == 0, own_ref[...].astype(F32), 0.0)
+    out_ref[...] = own + along_ref[...].astype(F32)
+
+
+def finish_kernel(begun_ref, aside_ref, relayed_ref, out_ref):
+    out_ref[...] = begun_ref[...] + aside_ref[...].astype(F32) + relayed_ref[...].astype(F32)
+
+
+def gather_call(kernel, *pieces):
+    return pl.pallas_call(
+        kernel,
+        in_specs=[VMEM] * len(pieces),
         out_specs=VMEM,
-        out_shape=pltpu.VMEM(own.shape, F32),
+        out_shape=pltpu.VMEM(pieces[0].shape, F32),
         compiler_params=pltpu.CompilerParams(vmem_limit_bytes=4 * 2**20),
         name="sum_chips",
-    )(on_chip(own), *[on_chip(p) for p in pieces])
+    )(*[on_chip(p) for p in pieces])
 
 
 def widen_kernel(picks, *refs):
@@ -257,14 +261,17 @@
 
     sends = {}
     halves = ((0, 2), (1, 3))
-    received = [lax.ppermute(back_call(fitted, tiles, 1, picks), "dp", swap) for picks in halves]
+    received = [lax.ppermute(back_call(fitted, tiles, 1, picks)[0], "dp", swap) for picks in halves]
     for picks, r in zip(halves, received):
-        sends.update(zip(picks, add_call(back_call(fitted, tiles, 0, picks), r, len(picks))))
+        sends.update(zip(picks, back_call(fitted, tiles, 0, picks, r)))
     hops = [tuple(row[j] for row in OFFSETS) for j in range(SETS)]
-    (relayed,) = add_call(sends[1], exchange(sends[0], RELAY), 1)
-    pieces = [exchange(x, h) for x, h in zip((sends[3], sends[2], relayed), hops[:0:-1])]
-    partial = gather_call(sends[3], pieces)
-    (full,) = add_call(partial, lax.ppermute(partial, "dp", swap), 1)
+    relay = exchange(sends[0], RELAY)
+    along = exchange(sends[2], hops[2])
+    aside = exchange(sends[3], hops[3])
+    relayed = add_call(sends[1], relay)
+    begun = gather_call(begin_kernel, sends[3], along)
+    partial = gather_call(finish_kernel, begun, aside, exchange(relayed, hops[1]))
+    full = add_call(partial, lax.ppermute(partial, "dp", swap))
     pieces = [exchange(full, h) for h in hops[1:]]
     pieces = [exchange(pieces[0], RELAY)] + pieces
     others = [None] + [lax.ppermute(p, "dp", swap) for p in pieces[1:]]

time: 93.9 us -> 92.6 us (0.986)
  waiting for transfers between devices: 14.3 us -> 11.7 us
  starting transfers between devices: 21.2 us -> 22.9 us
    ppermute x8, waiting for transfers between devices: 12.3 us -> 9.13 us  [exchange(): return lax.ppermute(x, 'dp', pairs)]
    ppermute x8, starting transfers between devices: 13 us -> 15.7 us  [exchange(): return lax.ppermute(x, 'dp', pairs)]
  transfers between devices with their start and end apart: 15 -> 15, of which waited for: 7 -> 9; matrix products, arithmetic and copies ran while one was open for 0% -> 0% of each run, Pallas kernels for 7% -> 7%
where the time goes in v4:
time: 92.6 us; the launch traced here: 92.4 us
  blocking collectives  32.5 us (35%)
  Pallas kernels  25.3 us (27%)
  starting transfers between devices  22.9 us (25%)
  waiting for transfers between devices  11.7 us (13%)
    all_to_all x1, blocking collectives, per_device(): lax.all_to_all(partial_fit.reshape(groups, part, WIDTH), 'center', 0, 0)  21.6 us
    pallas_call x1, Pallas kernels, fit_call(): pl.pallas_call(functools.partial(fit_kernel, tile_rows), grid=(count // c...  17 us
    ppermute x8, starting transfers between devices, exchange(): return lax.ppermute(x, 'dp', pairs)  15.7 us
    all_to_all x1, blocking collectives, per_device(): lax.all_to_all(sum_call(pieces), 'center', 0, 0).reshape(rows, WIDTH)  10.9 us
    ppermute x8, waiting for transfers between devices, exchange(): return lax.ppermute(x, 'dp', pairs)  9.13 us
    pallas_call x4, Pallas kernels, back_call(): pl.pallas_call(functools.partial(back_kernel, other, picks), in_specs=[VM...  4.52 us
    ppermute x3, starting transfers between devices, per_device(): others = [None] + [lax.ppermute(p, 'dp', swap) for p in pieces[1:]]  3.91 us
    pallas_call x3, Pallas kernels, widen_call(): pl.pallas_call(kernel, in_specs=[VMEM] * count + [hbm] * len(more), out_s...  3.42 us
  transfers between devices with their start and end apart: 15, of which 9 were waited for; matrix products, arithmetic and copies ran while one was open for 0% of the time, Pallas kernels for 7%

profile of v4, /device:TPU:1, one launch (start us, length us, event | category | flops | bytes accessed | tf_op | source)
XLA Modules:
  0.0 92.4 jit_solution(15945386291574127780)
XLA Ops:
  0.0 17.0 %fit_tiles.1 = (bf16[1536,8192]{1,0:T(8,128)(2,1)S(1)}, f32[1536,128]{1,0:T(8,128)S(1)}) custom-call(bf16[1536,128]{1,0:T(8,128)(2,1)} %points_ref.1, bf16[8192,128]{1,0:T(8,128)(2,1)} %centers_ref.1, f32[8192,128]{1,0:T(8,128)} %direction_ref.1), custom_call_target="tpu_custom_call" | custom-call | tf_op jit(solution)/shard_map/fit_tiles/pallas_call | solution.py:105
  17.0 21.6 %all_to_all.10.in_ref = f32[8,192,128]{2,1,0:T(8,128)S(1)} all-to-all(f32[8,192,128]{2,1,0:T(8,128)S(1)} %bitcast.6), channel_id=1, replica_groups=mesh['dp'=16,'center'=8] {'center'}, dimensions={0} | all-to-all | bytes 1572864 | tf_op jit(solution)/shard_map/all_to_all | solution.py:259
  38.7 10.9 %all_to_all.11 = bf16[8,192,128]{2,1,0:T(8,128)(2,1)S(1)} all-to-all(bf16[8,192,128]{2,1,0:T(8,128)(2,1)S(1)} %sum_pieces.1), channel_id=1, replica_groups=mesh['dp'=16,'center'=8] {'center'}, dimensions={0} | all-to-all | bytes 786432 | tf_op jit(solution)/shard_map/all_to_all | solution.py:260
  49.6 1.1 %back_tiles.6 = bf16[2048,128]{1,0:T(8,128)(2,1)S(1)} custom-call(bf16[1536,128]{1,0:T(8,128)(2,1)S(1)} %bitcast.2, bf16[1536,8192]{1,0:T(8,128)(2,1)S(1)} %get-tuple-element.14.tile_ref), custom_call_target="tpu_custom_call" | custom-call | tf_op jit(solution)/shard_map/back_tiles/pallas_call | solution.py:147
  50.7 3.1 %collective-permute-start.1 = (bf16[2048,128]{1,0:T(8,128)(2,1)S(1)}, bf16[2048,128]{1,0:T(8,128)(2,1)S(1)}, u32[]{:S(2)}, u32[]{:S(2)}) collective-permute-start(bf16[2048,128]{1,0:T(8,128)(2,1)S(1)} %back_tiles.6), channel_id=1, source_target_pairs={{0,8},{8,0},{16,24},{24,16},{32,40},{40,32},{48,56},{56,48},{64,72... | collective-permute-start | bytes 1572872 | tf_op jit(solution)/shard_map/ppermute | solution.py:264
  53.8 1.1 %back_tiles.4 = bf16[2048,128]{1,0:T(8,128)(2,1)S(1)} custom-call(bf16[1536,128]{1,0:T(8,128)(2,1)S(1)} %bitcast.3, bf16[1536,8192]{1,0:T(8,128)(2,1)S(1)} %get-tuple-element.14.tile_ref), custom_call_target="tpu_custom_call" | custom-call | tf_op jit(solution)/shard_map/back_tiles/pallas_call | solution.py:147
  54.9 0.1 collective-permute-start
  55.0 0.3 collective-permute-done.1.refs_0_
  55.4 1.2 %back_tiles.7 = (bf16[1024,128]{1,0:T(8,128)(2,1)S(1)}, bf16[1024,128]{1,0:T(8,128)(2,1)S(1)}) custom-call(bf16[1536,128]{1,0:T(8,128)(2,1)S(1)} %bitcast.4, bf16[1536,8192]{1,0:T(8,128)(2,1)S(1)} %get-tuple-element.14.tile_ref, bf16[2048,128]{1,0:T(8,128)(2,1)S(1)} %collective-permute-done.1.refs_0_), custom_call_target="tpu_custom_call" | custom-call | tf_op jit(solution)/shard_map/back_tiles/pallas_call | solution.py:147
  56.5 2.6 %collective-permute-start.4 = (bf16[1024,128]{1,0:T(8,128)(2,1)S(1)}, bf16[1024,128]{1,0:T(8,128)(2,1)S(1)}, u32[]{:S(2)}, u32[]{:S(2)}) collective-permute-start(bf16[1024,128]{1,0:T(8,128)(2,1)S(1)} %get-tuple-element.18), channel_id=1, source_target_pairs={{0,32},{8,104},{16,48},{24,120},{32,0},{40,72},{48,16},{56,88},{64... | collective-permute-start | bytes 786440 | tf_op jit(solution)/shard_map/ppermute | solution.py:48
  59.1 0.7 collective-permute-start.2
  59.8 0.0 collective-permute-done.refs_0_
  59.8 1.1 %back_tiles.5 = (bf16[1024,128]{1,0:T(8,128)(2,1)S(1)}, bf16[1024,128]{1,0:T(8,128)(2,1)S(1)}) custom-call(bf16[1536,128]{1,0:T(8,128)(2,1)S(1)} %bitcast.5, bf16[1536,8192]{1,0:T(8,128)(2,1)S(1)} %get-tuple-element.14.tile_ref, bf16[2048,128]{1,0:T(8,128)(2,1)S(1)} %collective-permute-done.refs_0_), custom_call_target="tpu_custom_call" | custom-call | tf_op jit(solution)/shard_map/back_tiles/pallas_call | solution.py:147
  60.9 1.9 %collective-permute-start.3 = (bf16[1024,128]{1,0:T(8,128)(2,1)S(1)}, bf16[1024,128]{1,0:T(8,128)(2,1)S(1)}, u32[]{:S(2)}, u32[]{:S(2)}) collective-permute-start(bf16[1024,128]{1,0:T(8,128)(2,1)S(1)} %get-tuple-element.15.own_ref), channel_id=1, source_target_pairs={{8,40},{24,56},{40,8},{56,24},{72,104},{88,120},{104,72},{120,88},... | collective-permute-start | bytes 786440 | tf_op jit(solution)/shard_map/ppermute | solution.py:48
  62.8 0.2 collective-permute-done.4.b_ref
  63.0 0.1 add_pieces.2
  63.1 1.8 %collective-permute-start.5 = (bf16[1024,128]{1,0:T(8,128)(2,1)S(1)}, bf16[1024,128]{1,0:T(8,128)(2,1)S(1)}, u32[]{:S(2)}, u32[]{:S(2)}) collective-permute-start(bf16[1024,128]{1,0:T(8,128)(2,1)S(1)} %add_pieces.2), channel_id=1, source_target_pairs={{0,96},{8,56},{16,112},{24,40},{32,64},{40,24},{48,80},{56,8},{64,... | collective-permute-start | bytes 786440 | tf_op jit(solution)/shard_map/ppermute | solution.py:48
  64.9 1.7 %collective-permute-done.2.along_ref = bf16[1024,128]{1,0:T(8,128)(2,1)S(1)} collective-permute-done((bf16[1024,128]{1,0:T(8,128)(2,1)S(1)}, bf16[1024,128]{1,0:T(8,128)(2,1)S(1)}, u32[]{:S(2)}, u32[]{:S(2)}) %collective-permute-start.2) | collective-permute-done | bytes 262176 | tf_op jit(solution)/shard_map/ppermute | solution.py:48
  66.5 0.1 sum_chips.2.begun_ref
  66.6 1.7 %collective-permute-done.3.aside_ref = bf16[1024,128]{1,0:T(8,128)(2,1)S(1)} collective-permute-done((bf16[1024,128]{1,0:T(8,128)(2,1)S(1)}, bf16[1024,128]{1,0:T(8,128)(2,1)S(1)}, u32[]{:S(2)}, u32[]{:S(2)}) %collective-permute-start.3) | collective-permute-done | bytes 262176 | tf_op jit(solution)/shard_map/ppermute | solution.py:48
  68.3 2.9 %collective-permute-done.5.relayed_ref = bf16[1024,128]{1,0:T(8,128)(2,1)S(1)} collective-permute-done((bf16[1024,128]{1,0:T(8,128)(2,1)S(1)}, bf16[1024,128]{1,0:T(8,128)(2,1)S(1)}, u32[]{:S(2)}, u32[]{:S(2)}) %collective-permute-start.5) | collective-permute-done | bytes 262176 | tf_op jit(solution)/shard_map/ppermute | solution.py:48
  71.2 0.1 sum_chips.3.a_ref
  71.3 0.1 collective-permute-start.6
  71.4 1.9 %collective-permute-done.6.b_ref = f32[1024,128]{1,0:T(8,128)S(1)} collective-permute-done((f32[1024,128]{1,0:T(8,128)S(1)}, f32[1024,128]{1,0:T(8,128)S(1)}, u32[]{:S(2)}, u32[]{:S(2)}) %collective-permute-start.6) | collective-permute-done | bytes 524320 | tf_op jit(solution)/shard_map/ppermute | solution.py:274
  73.4 0.6 collective-permute-start.7
  73.9 2.9 %collective-permute-start.9 = (bf16[1024,128]{1,0:T(8,128)(2,1)S(1)}, bf16[1024,128]{1,0:T(8,128)(2,1)S(1)}, u32[]{:S(2)}, u32[]{:S(2)}) collective-permute-start(bf16[1024,128]{1,0:T(8,128)(2,1)S(1)} %add_pieces.3.refs_0_), channel_id=1, source_target_pairs={{0,16},{8,120},{16,0},{24,104},{32,48},{40,88},{48,32},{56,72},{64... | collective-permute-start | bytes 786440 | tf_op jit(solution)/shard_map/ppermute | solution.py:48
  76.8 2.7 %collective-permute-start.10 = (bf16[1024,128]{1,0:T(8,128)(2,1)S(1)}, bf16[1024,128]{1,0:T(8,128)(2,1)S(1)}, u32[]{:S(2)}, u32[]{:S(2)}) collective-permute-start(bf16[1024,128]{1,0:T(8,128)(2,1)S(1)} %add_pieces.3.refs_0_), channel_id=1, source_target_pairs={{8,40},{24,56},{40,8},{56,24},{72,104},{88,120},{104,72},{120,88},... | collective-permute-start | bytes 786440 | tf_op jit(solution)/shard_map/ppermute | solution.py:48
  79.6 0.6 collective-permute-done.7.refs_1_
  80.2 3.4 %collective-permute-start.11 = (bf16[1024,128]{1,0:T(8,128)(2,1)S(1)}, bf16[1024,128]{1,0:T(8,128)(2,1)S(1)}, u32[]{:S(2)}, u32[]{:S(2)}) collective-permute-start(bf16[1024,128]{1,0:T(8,128)(2,1)S(1)} %collective-permute-done.7.refs_1_), channel_id=1, source_target_pairs={{0,8},{8,0},{16,24},{24,16},{32,40},{40,32},{48,56},{56,48},{64,72... | collective-permute-start | bytes 786440 | tf_op jit(solution)/shard_map/ppermute | solution.py:277
  83.6 2.5 %collective-permute-start.8 = (bf16[1024,128]{1,0:T(8,128)(2,1)S(1)}, bf16[1024,128]{1,0:T(8,128)(2,1)S(1)}, u32[]{:S(2)}, u32[]{:S(2)}) collective-permute-start(bf16[1024,128]{1,0:T(8,128)(2,1)S(1)} %collective-permute-done.7.refs_1_), channel_id=1, source_target_pairs={{0,32},{8,104},{16,48},{24,120},{32,0},{40,72},{48,16},{56,88},{64... | collective-permute-start | bytes 786440 | tf_op jit(solution)/shard_map/ppermute | solution.py:48
  86.1 0.0 collective-permute-done.9.refs_2_
  86.2 0.0 collective-permute-start.13
  86.2 0.0 collective-permute-done.10.refs_3_
  86.2 0.5 collective-permute-start.14
  86.7 0.0 collective-permute-done.11.refs_4_
  86.7 1.4 %widen.3.refs_4_ = f32[8192,128]{1,0:T(8,128)} custom-call(bf16[1024,128]{1,0:T(8,128)(2,1)S(1)} %add_pieces.3.refs_0_, bf16[1024,128]{1,0:T(8,128)(2,1)S(1)} %collective-permute-done.7.refs_1_, bf16[1024,128]{1,0:T(8,128)(2,1)S(1)} %collective-permute-done.9.refs_2_, bf16[1024,128]{1,0:T(8,128)(2,1)S(1)} %collective-permute-done.10.refs_3_, ...), custom_call_target="tpu_custom_call" | custom-call | tf_op jit(solution)/shard_map/widen/pallas_call | solution.py:240
  88.1 2.0 %collective-permute-done.8.refs_3_ = bf16[1024,128]{1,0:T(8,128)(2,1)S(1)} collective-permute-done((bf16[1024,128]{1,0:T(8,128)(2,1)S(1)}, bf16[1024,128]{1,0:T(8,128)(2,1)S(1)}, u32[]{:S(2)}, u32[]{:S(2)}) %collective-permute-start.8) | collective-permute-done | bytes 262176 | tf_op jit(solution)/shard_map/ppermute | solution.py:48
  90.1 0.0 collective-permute-start.12
  90.1 0.0 collective-permute-done.13.refs_1_
  90.1 0.0 collective-permute-done.14.refs_2_
  90.1 1.2 %widen.4.refs_2_ = f32[8192,128]{1,0:T(8,128)} custom-call(bf16[1024,128]{1,0:T(8,128)(2,1)S(1)} %add_pieces.3.refs_0_, bf16[1024,128]{1,0:T(8,128)(2,1)S(1)} %collective-permute-done.13.refs_1_, bf16[1024,128]{1,0:T(8,128)(2,1)S(1)} %collective-permute-done.14.refs_2_, ...), custom_call_target="tpu_custom_call", output_to_operand_aliasing={{}: (4, {})} | custom-call | tf_op jit(solution)/shard_map/widen/pallas_call | solution.py:240
  91.3 0.3 collective-permute-done.12.refs_1_
  91.6 0.8 widen.5
  (2 shorter events, 0.1 us)
Async XLA Ops:
  50.7 4.7 %collective-permute-start.1 = (bf16[2048,128]{1,0:T(8,128)(2,1)S(1)}, bf16[2048,128]{1,0:T(8,128)(2,1)S(1)}, u32[]{:S(2)}, u32[]{:S(2)}) collective-permute-start(bf16[2048,128]{1,0:T(8,128)(2,1)S(1)} %back_tiles.6), channel_id=1, source_target_pairs={{0,8},{8,0},{16,24},{24,16},{32,40},{40,32},{48,56},{56,48},{64,72... | collective-permute-start | bytes 1572872 | tf_op jit(solution)/shard_map/ppermute | solution.py:264
  54.9 4.8 %collective-permute-start = (bf16[2048,128]{1,0:T(8,128)(2,1)S(1)}, bf16[2048,128]{1,0:T(8,128)(2,1)S(1)}, u32[]{:S(2)}, u32[]{:S(2)}) collective-permute-start(bf16[2048,128]{1,0:T(8,128)(2,1)S(1)} %back_tiles.4), channel_id=1, source_target_pairs={{0,8},{8,0},{16,24},{24,16},{32,40},{40,32},{48,56},{56,48},{64,72... | collective-permute-start | bytes 1572872 | tf_op jit(solution)/shard_map/ppermute | solution.py:264
  56.5 6.5 %collective-permute-start.4 = (bf16[1024,128]{1,0:T(8,128)(2,1)S(1)}, bf16[1024,128]{1,0:T(8,128)(2,1)S(1)}, u32[]{:S(2)}, u32[]{:S(2)}) collective-permute-start(bf16[1024,128]{1,0:T(8,128)(2,1)S(1)} %get-tuple-element.18), channel_id=1, source_target_pairs={{0,32},{8,104},{16,48},{24,120},{32,0},{40,72},{48,16},{56,88},{64... | collective-permute-start | bytes 786440 | tf_op jit(solution)/shard_map/ppermute | solution.py:48
  59.1 7.4 %collective-permute-start.2 = (bf16[1024,128]{1,0:T(8,128)(2,1)S(1)}, bf16[1024,128]{1,0:T(8,128)(2,1)S(1)}, u32[]{:S(2)}, u32[]{:S(2)}) collective-permute-start(bf16[1024,128]{1,0:T(8,128)(2,1)S(1)} %get-tuple-element.16), channel_id=1, source_target_pairs={{0,16},{8,120},{16,0},{24,104},{32,48},{40,88},{48,32},{56,72},{64... | collective-permute-start | bytes 786440 | tf_op jit(solution)/shard_map/ppermute | solution.py:48
  60.9 7.4 %collective-permute-start.3 = (bf16[1024,128]{1,0:T(8,128)(2,1)S(1)}, bf16[1024,128]{1,0:T(8,128)(2,1)S(1)}, u32[]{:S(2)}, u32[]{:S(2)}) collective-permute-start(bf16[1024,128]{1,0:T(8,128)(2,1)S(1)} %get-tuple-element.15.own_ref), channel_id=1, source_target_pairs={{8,40},{24,56},{40,8},{56,24},{72,104},{88,120},{104,72},{120,88},... | collective-permute-start | bytes 786440 | tf_op jit(solution)/shard_map/ppermute | solution.py:48
  63.1 8.2 %collective-permute-start.5 = (bf16[1024,128]{1,0:T(8,128)(2,1)S(1)}, bf16[1024,128]{1,0:T(8,128)(2,1)S(1)}, u32[]{:S(2)}, u32[]{:S(2)}) collective-permute-start(bf16[1024,128]{1,0:T(8,128)(2,1)S(1)} %add_pieces.2), channel_id=1, source_target_pairs={{0,96},{8,56},{16,112},{24,40},{32,64},{40,24},{48,80},{56,8},{64,... | collective-permute-start | bytes 786440 | tf_op jit(solution)/shard_map/ppermute | solution.py:48
  71.3 2.0 %collective-permute-start.6 = (f32[1024,128]{1,0:T(8,128)S(1)}, f32[1024,128]{1,0:T(8,128)S(1)}, u32[]{:S(2)}, u32[]{:S(2)}) collective-permute-start(f32[1024,128]{1,0:T(8,128)S(1)} %sum_chips.3.a_ref), channel_id=1, source_target_pairs={{0,8},{8,0},{16,24},{24,16},{32,40},{40,32},{48,56},{56,48},{64,72... | collective-permute-start | bytes 1572872 | tf_op jit(solution)/shard_map/ppermute | solution.py:274
  73.4 6.9 %collective-permute-start.7 = (bf16[1024,128]{1,0:T(8,128)(2,1)S(1)}, bf16[1024,128]{1,0:T(8,128)(2,1)S(1)}, u32[]{:S(2)}, u32[]{:S(2)}) collective-permute-start(bf16[1024,128]{1,0:T(8,128)(2,1)S(1)} %add_pieces.3.refs_0_), channel_id=1, source_target_pairs={{0,96},{8,56},{16,112},{24,40},{32,64},{40,24},{48,80},{56,8},{64,... | collective-permute-start | bytes 786440 | tf_op jit(solution)/shard_map/ppermute | solution.py:48
  73.9 12.2 %collective-permute-start.9 = (bf16[1024,128]{1,0:T(8,128)(2,1)S(1)}, bf16[1024,128]{1,0:T(8,128)(2,1)S(1)}, u32[]{:S(2)}, u32[]{:S(2)}) collective-permute-start(bf16[1024,128]{1,0:T(8,128)(2,1)S(1)} %add_pieces.3.refs_0_), channel_id=1, source_target_pairs={{0,16},{8,120},{16,0},{24,104},{32,48},{40,88},{48,32},{56,72},{64... | collective-permute-start | bytes 786440 | tf_op jit(solution)/shard_map/ppermute | solution.py:48
  76.8 9.3 %collective-permute-start.10 = (bf16[1024,128]{1,0:T(8,128)(2,1)S(1)}, bf16[1024,128]{1,0:T(8,128)(2,1)S(1)}, u32[]{:S(2)}, u32[]{:S(2)}) collective-permute-start(bf16[1024,128]{1,0:T(8,128)(2,1)S(1)} %add_pieces.3.refs_0_), channel_id=1, source_target_pairs={{8,40},{24,56},{40,8},{56,24},{72,104},{88,120},{104,72},{120,88},... | collective-permute-start | bytes 786440 | tf_op jit(solution)/shard_map/ppermute | solution.py:48
  80.2 6.4 %collective-permute-start.11 = (bf16[1024,128]{1,0:T(8,128)(2,1)S(1)}, bf16[1024,128]{1,0:T(8,128)(2,1)S(1)}, u32[]{:S(2)}, u32[]{:S(2)}) collective-permute-start(bf16[1024,128]{1,0:T(8,128)(2,1)S(1)} %collective-permute-done.7.refs_1_), channel_id=1, source_target_pairs={{0,8},{8,0},{16,24},{24,16},{32,40},{40,32},{48,56},{56,48},{64,72... | collective-permute-start | bytes 786440 | tf_op jit(solution)/shard_map/ppermute | solution.py:277
  83.6 6.4 %collective-permute-start.8 = (bf16[1024,128]{1,0:T(8,128)(2,1)S(1)}, bf16[1024,128]{1,0:T(8,128)(2,1)S(1)}, u32[]{:S(2)}, u32[]{:S(2)}) collective-permute-start(bf16[1024,128]{1,0:T(8,128)(2,1)S(1)} %collective-permute-done.7.refs_1_), channel_id=1, source_target_pairs={{0,32},{8,104},{16,48},{24,120},{32,0},{40,72},{48,16},{56,88},{64... | collective-permute-start | bytes 786440 | tf_op jit(solution)/shard_map/ppermute | solution.py:48
  86.2 3.9 %collective-permute-start.13 = (bf16[1024,128]{1,0:T(8,128)(2,1)S(1)}, bf16[1024,128]{1,0:T(8,128)(2,1)S(1)}, u32[]{:S(2)}, u32[]{:S(2)}) collective-permute-start(bf16[1024,128]{1,0:T(8,128)(2,1)S(1)} %collective-permute-done.9.refs_2_), channel_id=1, source_target_pairs={{0,8},{8,0},{16,24},{24,16},{32,40},{40,32},{48,56},{56,48},{64,72... | collective-permute-start | bytes 786440 | tf_op jit(solution)/shard_map/ppermute | solution.py:277
  86.2 3.9 %collective-permute-start.14 = (bf16[1024,128]{1,0:T(8,128)(2,1)S(1)}, bf16[1024,128]{1,0:T(8,128)(2,1)S(1)}, u32[]{:S(2)}, u32[]{:S(2)}) collective-permute-start(bf16[1024,128]{1,0:T(8,128)(2,1)S(1)} %collective-permute-done.10.refs_3_), channel_id=1, source_target_pairs={{0,8},{8,0},{16,24},{24,16},{32,40},{40,32},{48,56},{56,48},{64,72... | collective-permute-start | bytes 786440 | tf_op jit(solution)/shard_map/ppermute | solution.py:277
  90.1 1.5 %collective-permute-start.12 = (bf16[1024,128]{1,0:T(8,128)(2,1)S(1)}, bf16[1024,128]{1,0:T(8,128)(2,1)S(1)}, u32[]{:S(2)}, u32[]{:S(2)}) collective-permute-start(bf16[1024,128]{1,0:T(8,128)(2,1)S(1)} %collective-permute-done.8.refs_3_), channel_id=1, source_target_pairs={{0,8},{8,0},{16,24},{24,16},{32,40},{40,32},{48,56},{56,48},{64,72... | collective-permute-start | bytes 786440 | tf_op jit(solution)/shard_map/ppermute | solution.py:288

commit v5 on v4

--- a/solution.py
+++ b/solution.py
@@ -56,67 +56,87 @@
     return pltpu.with_memory_space_constraint(x, pltpu.HBM)
 
 
-def fit_kernel(tile_rows, points_ref, centers_ref, direction_ref, tile_ref, fit_ref, scaled_ref, turned_ref, weights_ref, sum_ref):
-    step = pl.program_id(0)
-    rows = points_ref.shape[0]
-    cols = centers_ref.shape[0]
-
-    @pl.when(step == 0)
-    def _():
-        high, low = split_bf16(points_ref[...].astype(F32) * CROSS_SCALE)
-        scaled_ref[:, :WIDTH] = high
-        scaled_ref[:, WIDTH:] = low
-        sum_ref[...] = jnp.zeros_like(sum_ref)
-
-    turned = centers_ref[...].astype(F32).T
-    shift = jnp.sum(turned * turned, axis=0, keepdims=True) * (-GAMMA * LOG2E)
-    turned = turned.astype(BF16)
-    turned_ref[:WIDTH, :] = turned
-    turned_ref[WIDTH:, :] = turned
-    weights_ref[...] = direction_ref[...].astype(BF16)
-
-    def make(t):
+def fit_kernel(cols, tile_rows, lag, points_hbm, centers_hbm, direction_hbm, tile_ref, fit_ref, *scratch):
+    points_ref, centers_ref, direction_ref, scaled_ref, turned_ref, weights_ref, sum_ref, sems = scratch
+    rows, count = points_ref.shape[0], centers_ref.shape[0]
+    blocks = count // cols
+
+    def block(b):
+        return slice(b * cols, (b + 1) * cols)
+
+    load_points = pltpu.make_async_copy(points_hbm, points_ref, sems.at[2 * blocks])
+    load_points.start()
+    loads = []
+    for b in range(blocks):
+        pairs = ((centers_hbm, centers_ref), (direction_hbm, direction_ref))
+        for k, (source, target) in enumerate(pairs):
+            loads.append(pltpu.make_async_copy(source.at[block(b), :], target.at[block(b), :], sems.at[2 * b + k]))
+            loads[-1].start()
+
+    load_points.wait()
+    high, low = split_bf16(points_ref[...].astype(F32) * CROSS_SCALE)
+    scaled_ref[:, :WIDTH] = high
+    scaled_ref[:, WIDTH:] = low
+
+    def prepare(b):
+        loads[2 * b].wait()
+        turned = centers_ref[block(b), :].astype(F32).T
+        shift = jnp.sum(turned * turned, axis=0, keepdims=True) * (-GAMMA * LOG2E)
+        turned = turned.astype(BF16)
+        turned_ref[:WIDTH, block(b)] = turned
+        turned_ref[WIDTH:, block(b)] = turned
+        loads[2 * b + 1].wait()
+        weights_ref[block(b), :] = direction_ref[block(b), :].astype(BF16)
+        return shift
+
+    def make(b, t, shift):
         at = slice(t * tile_rows, (t + 1) * tile_rows)
-        cross = jnp.dot(scaled_ref[at, :], turned_ref[...], preferred_element_type=F32)
+        cross = jnp.dot(scaled_ref[at, :], turned_ref[:, block(b)], preferred_element_type=F32)
         tile = jnp.exp2(cross + shift).astype(BF16)
-        tile_ref[at, pl.ds(pl.multiple_of(step * cols, cols), cols)] = tile
+        tile_ref[at, block(b)] = tile
         return tile
 
-    def fit(t, tile):
+    def fit(b, t, tile):
         at = slice(t * tile_rows, (t + 1) * tile_rows)
-        sum_ref[at, :] += jnp.dot(tile, weights_ref[...], preferred_element_type=F32)
-
-    count = rows // tile_rows
+        part = jnp.dot(tile, weights_ref[block(b), :], preferred_element_type=F32)
+        if b == 0:
+            sum_ref[at, :] = part
+        else:
+            sum_ref[at, :] += part
+
+    steps = [(b, t) for b in range(blocks) for t in range(rows // tile_rows)]
     made = []
-    for t in range(count + 2):
-        if t < count:
-            made.append(make(t))
-        if t >= 2:
-            fit(t - 2, made[t - 2])
-
-    @pl.when(step == pl.num_programs(0) - 1)
-    def _():
-        factor = jnp.exp2(2.0 * LOG2E * (AMP - GAMMA * row_squares(points_ref[...])))
-        fit_ref[...] = sum_ref[...] * (factor * (1.0 / math.sqrt(CENTERS)))
-
-
-def fit_call(points, centers, direction, cols=2048, tile_rows=256):
+    shifts = [prepare(0)]
+    for n in range(len(steps) + lag):
+        if n < len(steps):
+            b, t = steps[n]
+            made.append(make(b, t, shifts[b]))
+            if t == 2 and b + 1 < blocks:
+                shifts.append(prepare(b + 1))
+        if n >= lag:
+            fit(*steps[n - lag], made[n - lag])
+
+    factor = jnp.exp2(2.0 * LOG2E * (AMP - GAMMA * row_squares(points_ref[...])))
+    fit_ref[...] = sum_ref[...] * (factor * (1.0 / math.sqrt(CENTERS)))
+
+
+def fit_call(points, centers, direction, cols=4096, tile_rows=256, lag=1):
     rows, count = points.shape[0], centers.shape[0]
-    return pl.pallas_call(
-        functools.partial(fit_kernel, tile_rows),
-        grid=(count // cols,),
-        in_specs=[
-            pl.BlockSpec((rows, WIDTH), lambda j: (0, 0)),
-            pl.BlockSpec((cols, WIDTH), lambda j: (j, 0)),
-            pl.BlockSpec((cols, WIDTH), lambda j: (j, 0)),
-        ],
+    hbm = pl.BlockSpec(memory_space=pl.ANY)
+    return pl.pallas_call(
+        functools.partial(fit_kernel, cols, tile_rows, lag),
+        in_specs=[hbm] * 3,
         out_specs=[VMEM, VMEM],
         out_shape=[pltpu.VMEM((rows, count), BF16), pltpu.VMEM((rows, WIDTH), F32)],
         scratch_shapes=[
+            pltpu.VMEM((rows, WIDTH), BF16),
+            pltpu.VMEM((count, WIDTH), BF16),
+            pltpu.VMEM((count, WIDTH), F32),
             pltpu.VMEM((rows, 2 * WIDTH), BF16),
-            pltpu.VMEM((2 * WIDTH, cols), BF16),
-            pltpu.VMEM((cols, WIDTH), BF16),
+            pltpu.VMEM((2 * WIDTH, count), BF16),
+            pltpu.VMEM((count, WIDTH), BF16),
             pltpu.VMEM((rows, WIDTH), F32),
+            pltpu.SemaphoreType.DMA((2 * (count // cols) + 1,)),
         ],
         compiler_params=pltpu.CompilerParams(vmem_limit_bytes=30 * 2**20),
         name="fit_tiles",
@@ -283,10 +303,10 @@
             chosen.append((other, j, (0 if j == 3 else len(parts) - 1, len(parts) - 1)))
         return widen_call(parts, chosen, out)
 
-    out = write(None, (0, 1), (0, 2), (0, 3), (1, 1))
+    out = write(None, (0, 1), (0, 3), (1, 1))
     pieces[0], out = lax.optimization_barrier((pieces[0], out))
     others[0] = lax.ppermute(pieces[0], "dp", swap)
-    out = write(out, (1, 2), (1, 3), (0, 0))
+    out = write(out, (0, 2), (1, 3), (1, 2), (0, 0))
     return write(out, (1, 0))
 
 

time: 92.6 us -> 90 us (0.972)
  waiting for transfers between devices: 11.7 us -> 10.1 us
    ppermute x3, starting transfers between devices: 3.91 us -> 2.36 us  [per_device(): others = [None] + [lax.ppermute(p, 'dp', swap) for p in pieces[1:]]]
    ppermute x8, waiting for transfers between devices: 9.13 us -> 7.74 us  [exchange(): return lax.ppermute(x, 'dp', pairs)]
where the time goes in v5:
time: 90 us; the launch traced here: 89.8 us
  blocking collectives  32.5 us (36%)
  Pallas kernels  24.9 us (28%)
  starting transfers between devices  22 us (24%)
  waiting for transfers between devices  10.1 us (11%)
    all_to_all x1, blocking collectives, per_device(): lax.all_to_all(partial_fit.reshape(groups, part, WIDTH), 'center', 0, 0)  21.6 us
    pallas_call x1, Pallas kernels, fit_call(): pl.pallas_call(functools.partial(fit_kernel, cols, tile_rows, lag), in_sp...  16.6 us
    ppermute x8, starting transfers between devices, exchange(): return lax.ppermute(x, 'dp', pairs)  16.3 us
    all_to_all x1, blocking collectives, per_device(): lax.all_to_all(sum_call(pieces), 'center', 0, 0).reshape(rows, WIDTH)  10.9 us
    ppermute x8, waiting for transfers between devices, exchange(): return lax.ppermute(x, 'dp', pairs)  7.74 us
    pallas_call x4, Pallas kernels, back_call(): pl.pallas_call(functools.partial(back_kernel, other, picks), in_specs=[VM...  4.51 us
    pallas_call x3, Pallas kernels, widen_call(): pl.pallas_call(kernel, in_specs=[VMEM] * count + [hbm] * len(more), out_s...  3.42 us
    ppermute x2, starting transfers between devices, per_device(): lax.ppermute(back_call(fitted, tiles, 1, picks)[0], 'dp', swap)  3.19 us
  transfers between devices with their start and end apart: 15, of which 9 were waited for; matrix products, arithmetic and copies ran while one was open for 0% of the time, Pallas kernels for 7%

profile of v5, /device:TPU:1, one launch (start us, length us, event | category | flops | bytes accessed | tf_op | source)
XLA Modules:
  0.0 89.8 jit_solution(2434593006105465870)
XLA Ops:
  0.0 16.6 %fit_tiles.1 = (bf16[1536,8192]{1,0:T(8,128)(2,1)S(1)}, f32[1536,128]{1,0:T(8,128)S(1)}) custom-call(bf16[1536,128]{1,0:T(8,128)(2,1)} %points_hbm.1, bf16[8192,128]{1,0:T(8,128)(2,1)} %centers_hbm.1, f32[8192,128]{1,0:T(8,128)} %direction_hbm.1), custom_call_target="tpu_custom_call" | custom-call | tf_op jit(solution)/shard_map/fit_tiles/pallas_call | solution.py:126
  16.7 21.6 %all_to_all.10.in_ref = f32[8,192,128]{2,1,0:T(8,128)S(1)} all-to-all(f32[8,192,128]{2,1,0:T(8,128)S(1)} %bitcast.6), channel_id=1, replica_groups=mesh['dp'=16,'center'=8] {'center'}, dimensions={0} | all-to-all | bytes 1572864 | tf_op jit(solution)/shard_map/all_to_all | solution.py:279
  38.3 10.9 %all_to_all.11 = bf16[8,192,128]{2,1,0:T(8,128)(2,1)S(1)} all-to-all(bf16[8,192,128]{2,1,0:T(8,128)(2,1)S(1)} %sum_pieces.1), channel_id=1, replica_groups=mesh['dp'=16,'center'=8] {'center'}, dimensions={0} | all-to-all | bytes 786432 | tf_op jit(solution)/shard_map/all_to_all | solution.py:280
  49.2 1.1 %back_tiles.6 = bf16[2048,128]{1,0:T(8,128)(2,1)S(1)} custom-call(bf16[1536,128]{1,0:T(8,128)(2,1)S(1)} %bitcast.2, bf16[1536,8192]{1,0:T(8,128)(2,1)S(1)} %get-tuple-element.14.tile_ref), custom_call_target="tpu_custom_call" | custom-call | tf_op jit(solution)/shard_map/back_tiles/pallas_call | solution.py:167
  50.4 3.1 %collective-permute-start.1 = (bf16[2048,128]{1,0:T(8,128)(2,1)S(1)}, bf16[2048,128]{1,0:T(8,128)(2,1)S(1)}, u32[]{:S(2)}, u32[]{:S(2)}) collective-permute-start(bf16[2048,128]{1,0:T(8,128)(2,1)S(1)} %back_tiles.6), channel_id=1, source_target_pairs={{0,8},{8,0},{16,24},{24,16},{32,40},{40,32},{48,56},{56,48},{64,72... | collective-permute-start | bytes 1572872 | tf_op jit(solution)/shard_map/ppermute | solution.py:284
  53.5 1.1 %back_tiles.4 = bf16[2048,128]{1,0:T(8,128)(2,1)S(1)} custom-call(bf16[1536,128]{1,0:T(8,128)(2,1)S(1)} %bitcast.3, bf16[1536,8192]{1,0:T(8,128)(2,1)S(1)} %get-tuple-element.14.tile_ref), custom_call_target="tpu_custom_call" | custom-call | tf_op jit(solution)/shard_map/back_tiles/pallas_call | solution.py:167
  54.6 0.1 collective-permute-start
  54.7 0.3 collective-permute-done.1.refs_0_
  55.0 1.1 %back_tiles.7 = (bf16[1024,128]{1,0:T(8,128)(2,1)S(1)}, bf16[1024,128]{1,0:T(8,128)(2,1)S(1)}) custom-call(bf16[1536,128]{1,0:T(8,128)(2,1)S(1)} %bitcast.4, bf16[1536,8192]{1,0:T(8,128)(2,1)S(1)} %get-tuple-element.14.tile_ref, bf16[2048,128]{1,0:T(8,128)(2,1)S(1)} %collective-permute-done.1.refs_0_), custom_call_target="tpu_custom_call" | custom-call | tf_op jit(solution)/shard_map/back_tiles/pallas_call | solution.py:167
  56.1 2.6 %collective-permute-start.4 = (bf16[1024,128]{1,0:T(8,128)(2,1)S(1)}, bf16[1024,128]{1,0:T(8,128)(2,1)S(1)}, u32[]{:S(2)}, u32[]{:S(2)}) collective-permute-start(bf16[1024,128]{1,0:T(8,128)(2,1)S(1)} %get-tuple-element.18), channel_id=1, source_target_pairs={{0,32},{8,104},{16,48},{24,120},{32,0},{40,72},{48,16},{56,88},{64... | collective-permute-start | bytes 786440 | tf_op jit(solution)/shard_map/ppermute | solution.py:48
  58.7 0.6 collective-permute-start.2
  59.4 0.0 collective-permute-done.refs_0_
  59.4 1.1 %back_tiles.5 = (bf16[1024,128]{1,0:T(8,128)(2,1)S(1)}, bf16[1024,128]{1,0:T(8,128)(2,1)S(1)}) custom-call(bf16[1536,128]{1,0:T(8,128)(2,1)S(1)} %bitcast.5, bf16[1536,8192]{1,0:T(8,128)(2,1)S(1)} %get-tuple-element.14.tile_ref, bf16[2048,128]{1,0:T(8,128)(2,1)S(1)} %collective-permute-done.refs_0_), custom_call_target="tpu_custom_call" | custom-call | tf_op jit(solution)/shard_map/back_tiles/pallas_call | solution.py:167
  60.5 1.9 %collective-permute-start.3 = (bf16[1024,128]{1,0:T(8,128)(2,1)S(1)}, bf16[1024,128]{1,0:T(8,128)(2,1)S(1)}, u32[]{:S(2)}, u32[]{:S(2)}) collective-permute-start(bf16[1024,128]{1,0:T(8,128)(2,1)S(1)} %get-tuple-element.15.own_ref), channel_id=1, source_target_pairs={{8,40},{24,56},{40,8},{56,24},{72,104},{88,120},{104,72},{120,88},... | collective-permute-start | bytes 786440 | tf_op jit(solution)/shard_map/ppermute | solution.py:48
  62.4 0.2 collective-permute-done.4.b_ref
  62.7 0.1 add_pieces.2
  62.7 1.8 %collective-permute-start.5 = (bf16[1024,128]{1,0:T(8,128)(2,1)S(1)}, bf16[1024,128]{1,0:T(8,128)(2,1)S(1)}, u32[]{:S(2)}, u32[]{:S(2)}) collective-permute-start(bf16[1024,128]{1,0:T(8,128)(2,1)S(1)} %add_pieces.2), channel_id=1, source_target_pairs={{0,96},{8,56},{16,112},{24,40},{32,64},{40,24},{48,80},{56,8},{64,... | collective-permute-start | bytes 786440 | tf_op jit(solution)/shard_map/ppermute | solution.py:48
  64.5 1.7 %collective-permute-done.2.along_ref = bf16[1024,128]{1,0:T(8,128)(2,1)S(1)} collective-permute-done((bf16[1024,128]{1,0:T(8,128)(2,1)S(1)}, bf16[1024,128]{1,0:T(8,128)(2,1)S(1)}, u32[]{:S(2)}, u32[]{:S(2)}) %collective-permute-start.2) | collective-permute-done | bytes 262176 | tf_op jit(solution)/shard_map/ppermute | solution.py:48
  66.2 0.1 sum_chips.2.begun_ref
  66.2 1.7 %collective-permute-done.3.aside_ref = bf16[1024,128]{1,0:T(8,128)(2,1)S(1)} collective-permute-done((bf16[1024,128]{1,0:T(8,128)(2,1)S(1)}, bf16[1024,128]{1,0:T(8,128)(2,1)S(1)}, u32[]{:S(2)}, u32[]{:S(2)}) %collective-permute-start.3) | collective-permute-done | bytes 262176 | tf_op jit(solution)/shard_map/ppermute | solution.py:48
  67.9 2.9 %collective-permute-done.5.relayed_ref = bf16[1024,128]{1,0:T(8,128)(2,1)S(1)} collective-permute-done((bf16[1024,128]{1,0:T(8,128)(2,1)S(1)}, bf16[1024,128]{1,0:T(8,128)(2,1)S(1)}, u32[]{:S(2)}, u32[]{:S(2)}) %collective-permute-start.5) | collective-permute-done | bytes 262176 | tf_op jit(solution)/shard_map/ppermute | solution.py:48
  70.9 0.1 sum_chips.3.a_ref
  71.0 0.1 collective-permute-start.6
  71.0 1.9 %collective-permute-done.6.b_ref = f32[1024,128]{1,0:T(8,128)S(1)} collective-permute-done((f32[1024,128]{1,0:T(8,128)S(1)}, f32[1024,128]{1,0:T(8,128)S(1)}, u32[]{:S(2)}, u32[]{:S(2)}) %collective-permute-start.6) | collective-permute-done | bytes 524320 | tf_op jit(solution)/shard_map/ppermute | solution.py:294
  73.0 0.6 collective-permute-start.7
  73.6 3.4 %collective-permute-start.9 = (bf16[1024,128]{1,0:T(8,128)(2,1)S(1)}, bf16[1024,128]{1,0:T(8,128)(2,1)S(1)}, u32[]{:S(2)}, u32[]{:S(2)}) collective-permute-start(bf16[1024,128]{1,0:T(8,128)(2,1)S(1)} %add_pieces.3.refs_0_), channel_id=1, source_target_pairs={{8,40},{24,56},{40,8},{56,24},{72,104},{88,120},{104,72},{120,88},... | collective-permute-start | bytes 786440 | tf_op jit(solution)/shard_map/ppermute | solution.py:48
  76.9 3.0 %collective-permute-start.12 = (bf16[1024,128]{1,0:T(8,128)(2,1)S(1)}, bf16[1024,128]{1,0:T(8,128)(2,1)S(1)}, u32[]{:S(2)}, u32[]{:S(2)}) collective-permute-start(bf16[1024,128]{1,0:T(8,128)(2,1)S(1)} %add_pieces.3.refs_0_), channel_id=1, source_target_pairs={{0,16},{8,120},{16,0},{24,104},{32,48},{40,88},{48,32},{56,72},{64... | collective-permute-start | bytes 786440 | tf_op jit(solution)/shard_map/ppermute | solution.py:48
  79.9 0.0 collective-permute-done.7.refs_1_
  79.9 0.9 collective-permute-start.10
  80.8 2.5 %collective-permute-start.8 = (bf16[1024,128]{1,0:T(8,128)(2,1)S(1)}, bf16[1024,128]{1,0:T(8,128)(2,1)S(1)}, u32[]{:S(2)}, u32[]{:S(2)}) collective-permute-start(bf16[1024,128]{1,0:T(8,128)(2,1)S(1)} %collective-permute-done.7.refs_1_), channel_id=1, source_target_pairs={{0,32},{8,104},{16,48},{24,120},{32,0},{40,72},{48,16},{56,88},{64... | collective-permute-start | bytes 786440 | tf_op jit(solution)/shard_map/ppermute | solution.py:48
  83.3 0.0 collective-permute-done.9.refs_2_
  83.3 0.0 collective-permute-start.13
  83.3 1.1 %collective-permute-done.12.refs_1_ = bf16[1024,128]{1,0:T(8,128)(2,1)S(1)} collective-permute-done((bf16[1024,128]{1,0:T(8,128)(2,1)S(1)}, bf16[1024,128]{1,0:T(8,128)(2,1)S(1)}, u32[]{:S(2)}, u32[]{:S(2)}) %collective-permute-start.12) | collective-permute-done | bytes 262176 | tf_op jit(solution)/shard_map/ppermute | solution.py:48
  84.4 1.5 %collective-permute-start.14 = (bf16[1024,128]{1,0:T(8,128)(2,1)S(1)}, bf16[1024,128]{1,0:T(8,128)(2,1)S(1)}, u32[]{:S(2)}, u32[]{:S(2)}) collective-permute-start(bf16[1024,128]{1,0:T(8,128)(2,1)S(1)} %collective-permute-done.12.refs_1_), channel_id=1, source_target_pairs={{0,8},{8,0},{16,24},{24,16},{32,40},{40,32},{48,56},{56,48},{64,72... | collective-permute-start | bytes 786440 | tf_op jit(solution)/shard_map/ppermute | solution.py:297
  85.9 0.0 collective-permute-done.10.refs_3_
  85.9 1.2 %widen.3.refs_5_ = f32[8192,128]{1,0:T(8,128)} custom-call(bf16[1024,128]{1,0:T(8,128)(2,1)S(1)} %add_pieces.3.refs_0_, bf16[1024,128]{1,0:T(8,128)(2,1)S(1)} %collective-permute-done.7.refs_1_, bf16[1024,128]{1,0:T(8,128)(2,1)S(1)} %collective-permute-done.9.refs_2_, bf16[1024,128]{1,0:T(8,128)(2,1)S(1)} %collective-permute-done.10.refs_3_), custom_call_target="tpu_custom_call" | custom-call | tf_op jit(solution)/shard_map/widen/pallas_call | solution.py:260
  87.1 0.1 collective-permute-done.8.refs_4_
  87.2 0.0 collective-permute-start.11
  87.2 0.0 collective-permute-done.13.refs_2_
  87.2 0.0 collective-permute-done.14.refs_3_
  87.3 1.4 %widen.4.refs_2_ = f32[8192,128]{1,0:T(8,128)} custom-call(bf16[1024,128]{1,0:T(8,128)(2,1)S(1)} %add_pieces.3.refs_0_, bf16[1024,128]{1,0:T(8,128)(2,1)S(1)} %collective-permute-done.12.refs_1_, bf16[1024,128]{1,0:T(8,128)(2,1)S(1)} %collective-permute-done.13.refs_2_, ...), custom_call_target="tpu_custom_call", output_to_operand_aliasing={{}: (5, {})} | custom-call | tf_op jit(solution)/shard_map/widen/pallas_call | solution.py:260
  88.6 0.1 collective-permute-done.11.refs_1_
  88.8 0.8 widen.5
  (2 shorter events, 0.1 us)
Async XLA Ops:
  50.4 4.6 %collective-permute-start.1 = (bf16[2048,128]{1,0:T(8,128)(2,1)S(1)}, bf16[2048,128]{1,0:T(8,128)(2,1)S(1)}, u32[]{:S(2)}, u32[]{:S(2)}) collective-permute-start(bf16[2048,128]{1,0:T(8,128)(2,1)S(1)} %back_tiles.6), channel_id=1, source_target_pairs={{0,8},{8,0},{16,24},{24,16},{32,40},{40,32},{48,56},{56,48},{64,72... | collective-permute-start | bytes 1572872 | tf_op jit(solution)/shard_map/ppermute | solution.py:284
  54.6 4.8 %collective-permute-start = (bf16[2048,128]{1,0:T(8,128)(2,1)S(1)}, bf16[2048,128]{1,0:T(8,128)(2,1)S(1)}, u32[]{:S(2)}, u32[]{:S(2)}) collective-permute-start(bf16[2048,128]{1,0:T(8,128)(2,1)S(1)} %back_tiles.4), channel_id=1, source_target_pairs={{0,8},{8,0},{16,24},{24,16},{32,40},{40,32},{48,56},{56,48},{64,72... | collective-permute-start | bytes 1572872 | tf_op jit(solution)/shard_map/ppermute | solution.py:284
  56.1 6.5 %collective-permute-start.4 = (bf16[1024,128]{1,0:T(8,128)(2,1)S(1)}, bf16[1024,128]{1,0:T(8,128)(2,1)S(1)}, u32[]{:S(2)}, u32[]{:S(2)}) collective-permute-start(bf16[1024,128]{1,0:T(8,128)(2,1)S(1)} %get-tuple-element.18), channel_id=1, source_target_pairs={{0,32},{8,104},{16,48},{24,120},{32,0},{40,72},{48,16},{56,88},{64... | collective-permute-start | bytes 786440 | tf_op jit(solution)/shard_map/ppermute | solution.py:48
  58.7 7.4 %collective-permute-start.2 = (bf16[1024,128]{1,0:T(8,128)(2,1)S(1)}, bf16[1024,128]{1,0:T(8,128)(2,1)S(1)}, u32[]{:S(2)}, u32[]{:S(2)}) collective-permute-start(bf16[1024,128]{1,0:T(8,128)(2,1)S(1)} %get-tuple-element.16), channel_id=1, source_target_pairs={{0,16},{8,120},{16,0},{24,104},{32,48},{40,88},{48,32},{56,72},{64... | collective-permute-start | bytes 786440 | tf_op jit(solution)/shard_map/ppermute | solution.py:48
  60.5 7.4 %collective-permute-start.3 = (bf16[1024,128]{1,0:T(8,128)(2,1)S(1)}, bf16[1024,128]{1,0:T(8,128)(2,1)S(1)}, u32[]{:S(2)}, u32[]{:S(2)}) collective-permute-start(bf16[1024,128]{1,0:T(8,128)(2,1)S(1)} %get-tuple-element.15.own_ref), channel_id=1, source_target_pairs={{8,40},{24,56},{40,8},{56,24},{72,104},{88,120},{104,72},{120,88},... | collective-permute-start | bytes 786440 | tf_op jit(solution)/shard_map/ppermute | solution.py:48
  62.7 8.2 %collective-permute-start.5 = (bf16[1024,128]{1,0:T(8,128)(2,1)S(1)}, bf16[1024,128]{1,0:T(8,128)(2,1)S(1)}, u32[]{:S(2)}, u32[]{:S(2)}) collective-permute-start(bf16[1024,128]{1,0:T(8,128)(2,1)S(1)} %add_pieces.2), channel_id=1, source_target_pairs={{0,96},{8,56},{16,112},{24,40},{32,64},{40,24},{48,80},{56,8},{64,... | collective-permute-start | bytes 786440 | tf_op jit(solution)/shard_map/ppermute | solution.py:48
  71.0 2.0 %collective-permute-start.6 = (f32[1024,128]{1,0:T(8,128)S(1)}, f32[1024,128]{1,0:T(8,128)S(1)}, u32[]{:S(2)}, u32[]{:S(2)}) collective-permute-start(f32[1024,128]{1,0:T(8,128)S(1)} %sum_chips.3.a_ref), channel_id=1, source_target_pairs={{0,8},{8,0},{16,24},{24,16},{32,40},{40,32},{48,56},{56,48},{64,72... | collective-permute-start | bytes 1572872 | tf_op jit(solution)/shard_map/ppermute | solution.py:294
  73.0 6.9 %collective-permute-start.7 = (bf16[1024,128]{1,0:T(8,128)(2,1)S(1)}, bf16[1024,128]{1,0:T(8,128)(2,1)S(1)}, u32[]{:S(2)}, u32[]{:S(2)}) collective-permute-start(bf16[1024,128]{1,0:T(8,128)(2,1)S(1)} %add_pieces.3.refs_0_), channel_id=1, source_target_pairs={{0,96},{8,56},{16,112},{24,40},{32,64},{40,24},{48,80},{56,8},{64,... | collective-permute-start | bytes 786440 | tf_op jit(solution)/shard_map/ppermute | solution.py:48
  73.6 9.7 %collective-permute-start.9 = (bf16[1024,128]{1,0:T(8,128)(2,1)S(1)}, bf16[1024,128]{1,0:T(8,128)(2,1)S(1)}, u32[]{:S(2)}, u32[]{:S(2)}) collective-permute-start(bf16[1024,128]{1,0:T(8,128)(2,1)S(1)} %add_pieces.3.refs_0_), channel_id=1, source_target_pairs={{8,40},{24,56},{40,8},{56,24},{72,104},{88,120},{104,72},{120,88},... | collective-permute-start | bytes 786440 | tf_op jit(solution)/shard_map/ppermute | solution.py:48
  76.9 7.5 %collective-permute-start.12 = (bf16[1024,128]{1,0:T(8,128)(2,1)S(1)}, bf16[1024,128]{1,0:T(8,128)(2,1)S(1)}, u32[]{:S(2)}, u32[]{:S(2)}) collective-permute-start(bf16[1024,128]{1,0:T(8,128)(2,1)S(1)} %add_pieces.3.refs_0_), channel_id=1, source_target_pairs={{0,16},{8,120},{16,0},{24,104},{32,48},{40,88},{48,32},{56,72},{64... | collective-permute-start | bytes 786440 | tf_op jit(solution)/shard_map/ppermute | solution.py:48
  79.9 6.0 %collective-permute-start.10 = (bf16[1024,128]{1,0:T(8,128)(2,1)S(1)}, bf16[1024,128]{1,0:T(8,128)(2,1)S(1)}, u32[]{:S(2)}, u32[]{:S(2)}) collective-permute-start(bf16[1024,128]{1,0:T(8,128)(2,1)S(1)} %collective-permute-done.7.refs_1_), channel_id=1, source_target_pairs={{0,8},{8,0},{16,24},{24,16},{32,40},{40,32},{48,56},{56,48},{64,72... | collective-permute-start | bytes 786440 | tf_op jit(solution)/shard_map/ppermute | solution.py:297
  80.8 6.4 %collective-permute-start.8 = (bf16[1024,128]{1,0:T(8,128)(2,1)S(1)}, bf16[1024,128]{1,0:T(8,128)(2,1)S(1)}, u32[]{:S(2)}, u32[]{:S(2)}) collective-permute-start(bf16[1024,128]{1,0:T(8,128)(2,1)S(1)} %collective-permute-done.7.refs_1_), channel_id=1, source_target_pairs={{0,32},{8,104},{16,48},{24,120},{32,0},{40,72},{48,16},{56,88},{64... | collective-permute-start | bytes 786440 | tf_op jit(solution)/shard_map/ppermute | solution.py:48
  83.3 3.9 %collective-permute-start.13 = (bf16[1024,128]{1,0:T(8,128)(2,1)S(1)}, bf16[1024,128]{1,0:T(8,128)(2,1)S(1)}, u32[]{:S(2)}, u32[]{:S(2)}) collective-permute-start(bf16[1024,128]{1,0:T(8,128)(2,1)S(1)} %collective-permute-done.9.refs_2_), channel_id=1, source_target_pairs={{0,8},{8,0},{16,24},{24,16},{32,40},{40,32},{48,56},{56,48},{64,72... | collective-permute-start | bytes 786440 | tf_op jit(solution)/shard_map/ppermute | solution.py:297
  84.4 2.8 %collective-permute-start.14 = (bf16[1024,128]{1,0:T(8,128)(2,1)S(1)}, bf16[1024,128]{1,0:T(8,128)(2,1)S(1)}, u32[]{:S(2)}, u32[]{:S(2)}) collective-permute-start(bf16[1024,128]{1,0:T(8,128)(2,1)S(1)} %collective-permute-done.12.refs_1_), channel_id=1, source_target_pairs={{0,8},{8,0},{16,24},{24,16},{32,40},{40,32},{48,56},{56,48},{64,72... | collective-permute-start | bytes 786440 | tf_op jit(solution)/shard_map/ppermute | solution.py:297
  87.2 1.5 %collective-permute-start.11 = (bf16[1024,128]{1,0:T(8,128)(2,1)S(1)}, bf16[1024,128]{1,0:T(8,128)(2,1)S(1)}, u32[]{:S(2)}, u32[]{:S(2)}) collective-permute-start(bf16[1024,128]{1,0:T(8,128)(2,1)S(1)} %collective-permute-done.8.refs_4_), channel_id=1, source_target_pairs={{0,8},{8,0},{16,24},{24,16},{32,40},{40,32},{48,56},{56,48},{64,72... | collective-permute-start | bytes 786440 | tf_op jit(solution)/shard_map/ppermute | solution.py:308

commit v6 on v5

--- a/solution.py
+++ b/solution.py
@@ -209,13 +209,15 @@
     )(on_chip(a), on_chip(b))
 
 
-def begin_kernel(own_ref, along_ref, out_ref):
+def begin_kernel(own_ref, along_ref, aside_ref, out_ref):
     own = jnp.where((lax.axis_index("dp") & 1) == 0, own_ref[...].astype(F32), 0.0)
-    out_ref[...] = own + along_ref[...].astype(F32)
-
-
-def finish_kernel(begun_ref, aside_ref, relayed_ref, out_ref):
-    out_ref[...] = begun_ref[...] + aside_ref[...].astype(F32) + relayed_ref[...].astype(F32)
+    out_ref[...] = own + along_ref[...].astype(F32) + aside_ref[...].astype(F32)
+
+
+def finish_kernel(begun_ref, begun_other_ref, last_ref, last_other_ref, out_ref):
+    total = begun_ref[...] + begun_other_ref[...]
+    total += last_ref[...].astype(F32) + last_other_ref[...].astype(F32)
+    out_ref[...] = total.astype(BF16)
 
 
 def gather_call(kernel, *pieces):
@@ -223,7 +225,7 @@
         kernel,
         in_specs=[VMEM] * len(pieces),
         out_specs=VMEM,
-        out_shape=pltpu.VMEM(pieces[0].shape, F32),
+        out_shape=pltpu.VMEM(pieces[0].shape, F32 if kernel is begin_kernel else BF16),
         compiler_params=pltpu.CompilerParams(vmem_limit_bytes=4 * 2**20),
         name="sum_chips",
     )(*[on_chip(p) for p in pieces])
@@ -289,9 +291,9 @@
     along = exchange(sends[2], hops[2])
     aside = exchange(sends[3], hops[3])
     relayed = add_call(sends[1], relay)
-    begun = gather_call(begin_kernel, sends[3], along)
-    partial = gather_call(finish_kernel, begun, aside, exchange(relayed, hops[1]))
-    full = add_call(partial, lax.ppermute(partial, "dp", swap))
+    begun = gather_call(begin_kernel, sends[3], along, aside)
+    last = exchange(relayed, hops[1])
+    full = gather_call(finish_kernel, begun, lax.ppermute(begun, "dp", swap), last, lax.ppermute(last, "dp", swap))
     pieces = [exchange(full, h) for h in hops[1:]]
     pieces = [exchange(pieces[0], RELAY)] + pieces
     others = [None] + [lax.ppermute(p, "dp", swap) for p in pieces[1:]]

time: 90 us -> 89.5 us (level)
    ppermute x1 -> x2, waiting for transfers between devices: 1.9 us -> 1.54 us  [the longest x1 1.53 us: per_device(): lax.ppermute(last, 'dp', swap)]
  transfers between devices with their start and end apart: 15 -> 16, of which waited for: 9 -> 9; matrix products, arithmetic and copies ran while one was open for 0% -> 0% of each run, Pallas kernels for 7% -> 7%
where the time goes in v6:
time: 89.5 us; the launch traced here: 89.3 us
  blocking collectives  32.5 us (36%)
  Pallas kernels  24.9 us (28%)
  starting transfers between devices  22 us (25%)
  waiting for transfers between devices  9.6 us (11%)
    all_to_all x1, blocking collectives, per_device(): lax.all_to_all(partial_fit.reshape(groups, part, WIDTH), 'center', 0, 0)  21.6 us
    pallas_call x1, Pallas kernels, fit_call(): pl.pallas_call(functools.partial(fit_kernel, cols, tile_rows, lag), in_sp...  16.6 us
    ppermute x8, starting transfers between devices, exchange(): return lax.ppermute(x, 'dp', pairs)  16.3 us
    all_to_all x1, blocking collectives, per_device(): lax.all_to_all(sum_call(pieces), 'center', 0, 0).reshape(rows, WIDTH)  10.9 us
    ppermute x8, waiting for transfers between devices, exchange(): return lax.ppermute(x, 'dp', pairs)  7.61 us
    pallas_call x4, Pallas kernels, back_call(): pl.pallas_call(functools.partial(back_kernel, other, picks), in_specs=[VM...  4.51 us
    pallas_call x3, Pallas kernels, widen_call(): pl.pallas_call(kernel, in_specs=[VMEM] * count + [hbm] * len(more), out_s...  3.42 us
    ppermute x2, starting transfers between devices, per_device(): lax.ppermute(back_call(fitted, tiles, 1, picks)[0], 'dp', swap)  3.19 us
  transfers between devices with their start and end apart: 16, of which 9 were waited for; matrix products, arithmetic and copies ran while one was open for 0% of the time, Pallas kernels for 7%

profile of v6, /device:TPU:1, one launch (start us, length us, event | category | flops | bytes accessed | tf_op | source)
XLA Modules:
  0.0 89.3 jit_solution(5296040996736691535)
XLA Ops:
  0.0 16.6 %fit_tiles.1 = (bf16[1536,8192]{1,0:T(8,128)(2,1)S(1)}, f32[1536,128]{1,0:T(8,128)S(1)}) custom-call(bf16[1536,128]{1,0:T(8,128)(2,1)} %points_hbm.1, bf16[8192,128]{1,0:T(8,128)(2,1)} %centers_hbm.1, f32[8192,128]{1,0:T(8,128)} %direction_hbm.1), custom_call_target="tpu_custom_call" | custom-call | tf_op jit(solution)/shard_map/fit_tiles/pallas_call | solution.py:126
  16.7 21.6 %all_to_all.10.in_ref = f32[8,192,128]{2,1,0:T(8,128)S(1)} all-to-all(f32[8,192,128]{2,1,0:T(8,128)S(1)} %bitcast.6), channel_id=1, replica_groups=mesh['dp'=16,'center'=8] {'center'}, dimensions={0} | all-to-all | bytes 1572864 | tf_op jit(solution)/shard_map/all_to_all | solution.py:281
  38.3 10.9 %all_to_all.11 = bf16[8,192,128]{2,1,0:T(8,128)(2,1)S(1)} all-to-all(bf16[8,192,128]{2,1,0:T(8,128)(2,1)S(1)} %sum_pieces.1), channel_id=1, replica_groups=mesh['dp'=16,'center'=8] {'center'}, dimensions={0} | all-to-all | bytes 786432 | tf_op jit(solution)/shard_map/all_to_all | solution.py:282
  49.2 1.1 %back_tiles.6 = bf16[2048,128]{1,0:T(8,128)(2,1)S(1)} custom-call(bf16[1536,128]{1,0:T(8,128)(2,1)S(1)} %bitcast.2, bf16[1536,8192]{1,0:T(8,128)(2,1)S(1)} %get-tuple-element.14.tile_ref), custom_call_target="tpu_custom_call" | custom-call | tf_op jit(solution)/shard_map/back_tiles/pallas_call | solution.py:167
  50.4 3.1 %collective-permute-start.1 = (bf16[2048,128]{1,0:T(8,128)(2,1)S(1)}, bf16[2048,128]{1,0:T(8,128)(2,1)S(1)}, u32[]{:S(2)}, u32[]{:S(2)}) collective-permute-start(bf16[2048,128]{1,0:T(8,128)(2,1)S(1)} %back_tiles.6), channel_id=1, source_target_pairs={{0,8},{8,0},{16,24},{24,16},{32,40},{40,32},{48,56},{56,48},{64,72... | collective-permute-start | bytes 1572872 | tf_op jit(solution)/shard_map/ppermute | solution.py:286
  53.5 1.1 %back_tiles.4 = bf16[2048,128]{1,0:T(8,128)(2,1)S(1)} custom-call(bf16[1536,128]{1,0:T(8,128)(2,1)S(1)} %bitcast.3, bf16[1536,8192]{1,0:T(8,128)(2,1)S(1)} %get-tuple-element.14.tile_ref), custom_call_target="tpu_custom_call" | custom-call | tf_op jit(solution)/shard_map/back_tiles/pallas_call | solution.py:167
  54.6 0.1 collective-permute-start
  54.7 0.3 collective-permute-done.1.refs_0_
  55.0 1.1 %back_tiles.7 = (bf16[1024,128]{1,0:T(8,128)(2,1)S(1)}, bf16[1024,128]{1,0:T(8,128)(2,1)S(1)}) custom-call(bf16[1536,128]{1,0:T(8,128)(2,1)S(1)} %bitcast.4, bf16[1536,8192]{1,0:T(8,128)(2,1)S(1)} %get-tuple-element.14.tile_ref, bf16[2048,128]{1,0:T(8,128)(2,1)S(1)} %collective-permute-done.1.refs_0_), custom_call_target="tpu_custom_call" | custom-call | tf_op jit(solution)/shard_map/back_tiles/pallas_call | solution.py:167
  56.1 2.6 %collective-permute-start.5 = (bf16[1024,128]{1,0:T(8,128)(2,1)S(1)}, bf16[1024,128]{1,0:T(8,128)(2,1)S(1)}, u32[]{:S(2)}, u32[]{:S(2)}) collective-permute-start(bf16[1024,128]{1,0:T(8,128)(2,1)S(1)} %get-tuple-element.18), channel_id=1, source_target_pairs={{0,32},{8,104},{16,48},{24,120},{32,0},{40,72},{48,16},{56,88},{64... | collective-permute-start | bytes 786440 | tf_op jit(solution)/shard_map/ppermute | solution.py:48
  58.7 0.6 collective-permute-start.2
  59.4 0.0 collective-permute-done.refs_0_
  59.4 1.1 %back_tiles.5 = (bf16[1024,128]{1,0:T(8,128)(2,1)S(1)}, bf16[1024,128]{1,0:T(8,128)(2,1)S(1)}) custom-call(bf16[1536,128]{1,0:T(8,128)(2,1)S(1)} %bitcast.5, bf16[1536,8192]{1,0:T(8,128)(2,1)S(1)} %get-tuple-element.14.tile_ref, bf16[2048,128]{1,0:T(8,128)(2,1)S(1)} %collective-permute-done.refs_0_), custom_call_target="tpu_custom_call" | custom-call | tf_op jit(solution)/shard_map/back_tiles/pallas_call | solution.py:167
  60.5 1.9 %collective-permute-start.3 = (bf16[1024,128]{1,0:T(8,128)(2,1)S(1)}, bf16[1024,128]{1,0:T(8,128)(2,1)S(1)}, u32[]{:S(2)}, u32[]{:S(2)}) collective-permute-start(bf16[1024,128]{1,0:T(8,128)(2,1)S(1)} %get-tuple-element.15.own_ref), channel_id=1, source_target_pairs={{8,40},{24,56},{40,8},{56,24},{72,104},{88,120},{104,72},{120,88},... | collective-permute-start | bytes 786440 | tf_op jit(solution)/shard_map/ppermute | solution.py:48
  62.4 0.2 collective-permute-done.5.b_ref
  62.7 0.1 add_pieces.1
  62.7 1.8 %collective-permute-start.6 = (bf16[1024,128]{1,0:T(8,128)(2,1)S(1)}, bf16[1024,128]{1,0:T(8,128)(2,1)S(1)}, u32[]{:S(2)}, u32[]{:S(2)}) collective-permute-start(bf16[1024,128]{1,0:T(8,128)(2,1)S(1)} %add_pieces.1), channel_id=1, source_target_pairs={{0,96},{8,56},{16,112},{24,40},{32,64},{40,24},{48,80},{56,8},{64,... | collective-permute-start | bytes 786440 | tf_op jit(solution)/shard_map/ppermute | solution.py:48
  64.5 1.7 %collective-permute-done.2.along_ref = bf16[1024,128]{1,0:T(8,128)(2,1)S(1)} collective-permute-done((bf16[1024,128]{1,0:T(8,128)(2,1)S(1)}, bf16[1024,128]{1,0:T(8,128)(2,1)S(1)}, u32[]{:S(2)}, u32[]{:S(2)}) %collective-permute-start.2) | collective-permute-done | bytes 262176 | tf_op jit(solution)/shard_map/ppermute | solution.py:48
  66.2 1.8 %collective-permute-done.3.aside_ref = bf16[1024,128]{1,0:T(8,128)(2,1)S(1)} collective-permute-done((bf16[1024,128]{1,0:T(8,128)(2,1)S(1)}, bf16[1024,128]{1,0:T(8,128)(2,1)S(1)}, u32[]{:S(2)}, u32[]{:S(2)}) %collective-permute-start.3) | collective-permute-done | bytes 262176 | tf_op jit(solution)/shard_map/ppermute | solution.py:48
  67.9 0.1 sum_chips.2.begun_ref
  68.0 0.1 collective-permute-start.4
  68.1 2.7 %collective-permute-done.6.last_ref = bf16[1024,128]{1,0:T(8,128)(2,1)S(1)} collective-permute-done((bf16[1024,128]{1,0:T(8,128)(2,1)S(1)}, bf16[1024,128]{1,0:T(8,128)(2,1)S(1)}, u32[]{:S(2)}, u32[]{:S(2)}) %collective-permute-start.6) | collective-permute-done | bytes 262176 | tf_op jit(solution)/shard_map/ppermute | solution.py:48
  70.9 0.0 collective-permute-start.7
  70.9 1.5 %collective-permute-done.7.last_other_ref = bf16[1024,128]{1,0:T(8,128)(2,1)S(1)} collective-permute-done((bf16[1024,128]{1,0:T(8,128)(2,1)S(1)}, bf16[1024,128]{1,0:T(8,128)(2,1)S(1)}, u32[]{:S(2)}, u32[]{:S(2)}) %collective-permute-start.7) | collective-permute-done | bytes 262176 | tf_op jit(solution)/shard_map/ppermute | solution.py:296
  72.4 0.0 collective-permute-done.4.begun_other_ref
  72.4 0.1 sum_chips.3.refs_0_
  72.5 0.6 collective-permute-start.8
  73.1 3.4 %collective-permute-start.10 = (bf16[1024,128]{1,0:T(8,128)(2,1)S(1)}, bf16[1024,128]{1,0:T(8,128)(2,1)S(1)}, u32[]{:S(2)}, u32[]{:S(2)}) collective-permute-start(bf16[1024,128]{1,0:T(8,128)(2,1)S(1)} %sum_chips.3.refs_0_), channel_id=1, source_target_pairs={{8,40},{24,56},{40,8},{56,24},{72,104},{88,120},{104,72},{120,88},... | collective-permute-start | bytes 786440 | tf_op jit(solution)/shard_map/ppermute | solution.py:48
  76.4 3.0 %collective-permute-start.13 = (bf16[1024,128]{1,0:T(8,128)(2,1)S(1)}, bf16[1024,128]{1,0:T(8,128)(2,1)S(1)}, u32[]{:S(2)}, u32[]{:S(2)}) collective-permute-start(bf16[1024,128]{1,0:T(8,128)(2,1)S(1)} %sum_chips.3.refs_0_), channel_id=1, source_target_pairs={{0,16},{8,120},{16,0},{24,104},{32,48},{40,88},{48,32},{56,72},{64... | collective-permute-start | bytes 786440 | tf_op jit(solution)/shard_map/ppermute | solution.py:48
  79.4 0.0 collective-permute-done.8.refs_1_
  79.4 0.9 collective-permute-start.11
  80.3 2.5 %collective-permute-start.9 = (bf16[1024,128]{1,0:T(8,128)(2,1)S(1)}, bf16[1024,128]{1,0:T(8,128)(2,1)S(1)}, u32[]{:S(2)}, u32[]{:S(2)}) collective-permute-start(bf16[1024,128]{1,0:T(8,128)(2,1)S(1)} %collective-permute-done.8.refs_1_), channel_id=1, source_target_pairs={{0,32},{8,104},{16,48},{24,120},{32,0},{40,72},{48,16},{56,88},{64... | collective-permute-start | bytes 786440 | tf_op jit(solution)/shard_map/ppermute | solution.py:48
  82.8 0.0 collective-permute-done.10.refs_2_
  82.8 0.0 collective-permute-start.14
  82.8 1.1 %collective-permute-done.13.refs_1_ = bf16[1024,128]{1,0:T(8,128)(2,1)S(1)} collective-permute-done((bf16[1024,128]{1,0:T(8,128)(2,1)S(1)}, bf16[1024,128]{1,0:T(8,128)(2,1)S(1)}, u32[]{:S(2)}, u32[]{:S(2)}) %collective-permute-start.13) | collective-permute-done | bytes 262176 | tf_op jit(solution)/shard_map/ppermute | solution.py:48
  84.0 1.5 %collective-permute-start.15 = (bf16[1024,128]{1,0:T(8,128)(2,1)S(1)}, bf16[1024,128]{1,0:T(8,128)(2,1)S(1)}, u32[]{:S(2)}, u32[]{:S(2)}) collective-permute-start(bf16[1024,128]{1,0:T(8,128)(2,1)S(1)} %collective-permute-done.13.refs_1_), channel_id=1, source_target_pairs={{0,8},{8,0},{16,24},{24,16},{32,40},{40,32},{48,56},{56,48},{64,72... | collective-permute-start | bytes 786440 | tf_op jit(solution)/shard_map/ppermute | solution.py:299
  85.4 0.0 collective-permute-done.11.refs_3_
  85.4 1.2 %widen.3.refs_5_ = f32[8192,128]{1,0:T(8,128)} custom-call(bf16[1024,128]{1,0:T(8,128)(2,1)S(1)} %sum_chips.3.refs_0_, bf16[1024,128]{1,0:T(8,128)(2,1)S(1)} %collective-permute-done.8.refs_1_, bf16[1024,128]{1,0:T(8,128)(2,1)S(1)} %collective-permute-done.10.refs_2_, bf16[1024,128]{1,0:T(8,128)(2,1)S(1)} %collective-permute-done.11.refs_3_), custom_call_target="tpu_custom_call" | custom-call | tf_op jit(solution)/shard_map/widen/pallas_call | solution.py:262
  86.7 0.1 collective-permute-done.9.refs_4_
  86.8 0.0 collective-permute-start.12
  86.8 0.0 collective-permute-done.14.refs_2_
  86.8 0.0 collective-permute-done.15.refs_3_
  86.8 1.4 %widen.4.refs_2_ = f32[8192,128]{1,0:T(8,128)} custom-call(bf16[1024,128]{1,0:T(8,128)(2,1)S(1)} %sum_chips.3.refs_0_, bf16[1024,128]{1,0:T(8,128)(2,1)S(1)} %collective-permute-done.13.refs_1_, bf16[1024,128]{1,0:T(8,128)(2,1)S(1)} %collective-permute-done.14.refs_2_, ...), custom_call_target="tpu_custom_call", output_to_operand_aliasing={{}: (5, {})} | custom-call | tf_op jit(solution)/shard_map/widen/pallas_call | solution.py:262
  88.2 0.1 collective-permute-done.12.refs_1_
  88.3 0.8 widen.5
  (1 shorter events, 0.0 us)
Async XLA Ops:
  50.4 4.6 %collective-permute-start.1 = (bf16[2048,128]{1,0:T(8,128)(2,1)S(1)}, bf16[2048,128]{1,0:T(8,128)(2,1)S(1)}, u32[]{:S(2)}, u32[]{:S(2)}) collective-permute-start(bf16[2048,128]{1,0:T(8,128)(2,1)S(1)} %back_tiles.6), channel_id=1, source_target_pairs={{0,8},{8,0},{16,24},{24,16},{32,40},{40,32},{48,56},{56,48},{64,72... | collective-permute-start | bytes 1572872 | tf_op jit(solution)/shard_map/ppermute | solution.py:286
  54.6 4.8 %collective-permute-start = (bf16[2048,128]{1,0:T(8,128)(2,1)S(1)}, bf16[2048,128]{1,0:T(8,128)(2,1)S(1)}, u32[]{:S(2)}, u32[]{:S(2)}) collective-permute-start(bf16[2048,128]{1,0:T(8,128)(2,1)S(1)} %back_tiles.4), channel_id=1, source_target_pairs={{0,8},{8,0},{16,24},{24,16},{32,40},{40,32},{48,56},{56,48},{64,72... | collective-permute-start | bytes 1572872 | tf_op jit(solution)/shard_map/ppermute | solution.py:286
  56.1 6.5 %collective-permute-start.5 = (bf16[1024,128]{1,0:T(8,128)(2,1)S(1)}, bf16[1024,128]{1,0:T(8,128)(2,1)S(1)}, u32[]{:S(2)}, u32[]{:S(2)}) collective-permute-start(bf16[1024,128]{1,0:T(8,128)(2,1)S(1)} %get-tuple-element.18), channel_id=1, source_target_pairs={{0,32},{8,104},{16,48},{24,120},{32,0},{40,72},{48,16},{56,88},{64... | collective-permute-start | bytes 786440 | tf_op jit(solution)/shard_map/ppermute | solution.py:48
  58.7 7.4 %collective-permute-start.2 = (bf16[1024,128]{1,0:T(8,128)(2,1)S(1)}, bf16[1024,128]{1,0:T(8,128)(2,1)S(1)}, u32[]{:S(2)}, u32[]{:S(2)}) collective-permute-start(bf16[1024,128]{1,0:T(8,128)(2,1)S(1)} %get-tuple-element.16), channel_id=1, source_target_pairs={{0,16},{8,120},{16,0},{24,104},{32,48},{40,88},{48,32},{56,72},{64... | collective-permute-start | bytes 786440 | tf_op jit(solution)/shard_map/ppermute | solution.py:48
  60.5 7.4 %collective-permute-start.3 = (bf16[1024,128]{1,0:T(8,128)(2,1)S(1)}, bf16[1024,128]{1,0:T(8,128)(2,1)S(1)}, u32[]{:S(2)}, u32[]{:S(2)}) collective-permute-start(bf16[1024,128]{1,0:T(8,128)(2,1)S(1)} %get-tuple-element.15.own_ref), channel_id=1, source_target_pairs={{8,40},{24,56},{40,8},{56,24},{72,104},{88,120},{104,72},{120,88},... | collective-permute-start | bytes 786440 | tf_op jit(solution)/shard_map/ppermute | solution.py:48
  62.7 8.2 %collective-permute-start.6 = (bf16[1024,128]{1,0:T(8,128)(2,1)S(1)}, bf16[1024,128]{1,0:T(8,128)(2,1)S(1)}, u32[]{:S(2)}, u32[]{:S(2)}) collective-permute-start(bf16[1024,128]{1,0:T(8,128)(2,1)S(1)} %add_pieces.1), channel_id=1, source_target_pairs={{0,96},{8,56},{16,112},{24,40},{32,64},{40,24},{48,80},{56,8},{64,... | collective-permute-start | bytes 786440 | tf_op jit(solution)/shard_map/ppermute | solution.py:48
  68.0 4.4 %collective-permute-start.4 = (f32[1024,128]{1,0:T(8,128)S(1)}, f32[1024,128]{1,0:T(8,128)S(1)}, u32[]{:S(2)}, u32[]{:S(2)}) collective-permute-start(f32[1024,128]{1,0:T(8,128)S(1)} %sum_chips.2.begun_ref), channel_id=1, source_target_pairs={{0,8},{8,0},{16,24},{24,16},{32,40},{40,32},{48,56},{56,48},{64,72... | collective-permute-start | bytes 1572872 | tf_op jit(solution)/shard_map/ppermute | solution.py:296
  70.9 1.5 %collective-permute-start.7 = (bf16[1024,128]{1,0:T(8,128)(2,1)S(1)}, bf16[1024,128]{1,0:T(8,128)(2,1)S(1)}, u32[]{:S(2)}, u32[]{:S(2)}) collective-permute-start(bf16[1024,128]{1,0:T(8,128)(2,1)S(1)} %collective-permute-done.6.last_ref), channel_id=1, source_target_pairs={{0,8},{8,0},{16,24},{24,16},{32,40},{40,32},{48,56},{56,48},{64,72... | collective-permute-start | bytes 786440 | tf_op jit(solution)/shard_map/ppermute | solution.py:296
  72.5 6.9 %collective-permute-start.8 = (bf16[1024,128]{1,0:T(8,128)(2,1)S(1)}, bf16[1024,128]{1,0:T(8,128)(2,1)S(1)}, u32[]{:S(2)}, u32[]{:S(2)}) collective-permute-start(bf16[1024,128]{1,0:T(8,128)(2,1)S(1)} %sum_chips.3.refs_0_), channel_id=1, source_target_pairs={{0,96},{8,56},{16,112},{24,40},{32,64},{40,24},{48,80},{56,8},{64,... | collective-permute-start | bytes 786440 | tf_op jit(solution)/shard_map/ppermute | solution.py:48
  73.1 9.7 %collective-permute-start.10 = (bf16[1024,128]{1,0:T(8,128)(2,1)S(1)}, bf16[1024,128]{1,0:T(8,128)(2,1)S(1)}, u32[]{:S(2)}, u32[]{:S(2)}) collective-permute-start(bf16[1024,128]{1,0:T(8,128)(2,1)S(1)} %sum_chips.3.refs_0_), channel_id=1, source_target_pairs={{8,40},{24,56},{40,8},{56,24},{72,104},{88,120},{104,72},{120,88},... | collective-permute-start | bytes 786440 | tf_op jit(solution)/shard_map/ppermute | solution.py:48
  76.4 7.5 %collective-permute-start.13 = (bf16[1024,128]{1,0:T(8,128)(2,1)S(1)}, bf16[1024,128]{1,0:T(8,128)(2,1)S(1)}, u32[]{:S(2)}, u32[]{:S(2)}) collective-permute-start(bf16[1024,128]{1,0:T(8,128)(2,1)S(1)} %sum_chips.3.refs_0_), channel_id=1, source_target_pairs={{0,16},{8,120},{16,0},{24,104},{32,48},{40,88},{48,32},{56,72},{64... | collective-permute-start | bytes 786440 | tf_op jit(solution)/shard_map/ppermute | solution.py:48
  79.4 6.0 %collective-permute-start.11 = (bf16[1024,128]{1,0:T(8,128)(2,1)S(1)}, bf16[1024,128]{1,0:T(8,128)(2,1)S(1)}, u32[]{:S(2)}, u32[]{:S(2)}) collective-permute-start(bf16[1024,128]{1,0:T(8,128)(2,1)S(1)} %collective-permute-done.8.refs_1_), channel_id=1, source_target_pairs={{0,8},{8,0},{16,24},{24,16},{32,40},{40,32},{48,56},{56,48},{64,72... | collective-permute-start | bytes 786440 | tf_op jit(solution)/shard_map/ppermute | solution.py:299
  80.3 6.4 %collective-permute-start.9 = (bf16[1024,128]{1,0:T(8,128)(2,1)S(1)}, bf16[1024,128]{1,0:T(8,128)(2,1)S(1)}, u32[]{:S(2)}, u32[]{:S(2)}) collective-permute-start(bf16[1024,128]{1,0:T(8,128)(2,1)S(1)} %collective-permute-done.8.refs_1_), channel_id=1, source_target_pairs={{0,32},{8,104},{16,48},{24,120},{32,0},{40,72},{48,16},{56,88},{64... | collective-permute-start | bytes 786440 | tf_op jit(solution)/shard_map/ppermute | solution.py:48
  82.8 3.9 %collective-permute-start.14 = (bf16[1024,128]{1,0:T(8,128)(2,1)S(1)}, bf16[1024,128]{1,0:T(8,128)(2,1)S(1)}, u32[]{:S(2)}, u32[]{:S(2)}) collective-permute-start(bf16[1024,128]{1,0:T(8,128)(2,1)S(1)} %collective-permute-done.10.refs_2_), channel_id=1, source_target_pairs={{0,8},{8,0},{16,24},{24,16},{32,40},{40,32},{48,56},{56,48},{64,72... | collective-permute-start | bytes 786440 | tf_op jit(solution)/shard_map/ppermute | solution.py:299
  84.0 2.8 %collective-permute-start.15 = (bf16[1024,128]{1,0:T(8,128)(2,1)S(1)}, bf16[1024,128]{1,0:T(8,128)(2,1)S(1)}, u32[]{:S(2)}, u32[]{:S(2)}) collective-permute-start(bf16[1024,128]{1,0:T(8,128)(2,1)S(1)} %collective-permute-done.13.refs_1_), channel_id=1, source_target_pairs={{0,8},{8,0},{16,24},{24,16},{32,40},{40,32},{48,56},{56,48},{64,72... | collective-permute-start | bytes 786440 | tf_op jit(solution)/shard_map/ppermute | solution.py:299
  86.8 1.5 %collective-permute-start.12 = (bf16[1024,128]{1,0:T(8,128)(2,1)S(1)}, bf16[1024,128]{1,0:T(8,128)(2,1)S(1)}, u32[]{:S(2)}, u32[]{:S(2)}) collective-permute-start(bf16[1024,128]{1,0:T(8,128)(2,1)S(1)} %collective-permute-done.9.refs_4_), channel_id=1, source_target_pairs={{0,8},{8,0},{16,24},{24,16},{32,40},{40,32},{48,56},{56,48},{64,72... | collective-permute-start | bytes 786440 | tf_op jit(solution)/shard_map/ppermute | solution.py:310
